TPU v7x, 256 devices: a whole 4x4x8 slice. The times are simulated.
256 devices in a mesh: dp: 8 (over z), ctx: 8 (over x_lo, y), tensor: 4 (over x_hi, core).
Axes of the slice: x: 4 (x_hi: 2, x_lo: 2; x = x_hi * 2 + x_lo), y: 4, z: 8, core: 2. Of those that a mesh axis runs over, the one named last changes fastest.
Arguments:
- tokens: bfloat16 [8192, 8192], P(('dp', 'ctx'), 'tensor'), may hold values from -6 to 6
- queries: bfloat16 [8192, 4096], P(('dp', 'ctx'), 'tensor'), may hold values from -110 to 110
- values: bfloat16 [8192, 512], P(('dp', 'ctx'), 'tensor'), may hold values from -6 to 6
- out_grad: bfloat16 [8192, 4096], P(('dp', 'ctx'), 'tensor'), may hold values from -6 to 6
- key_weight: bfloat16 [512, 8192], P(None, 'tensor'), may hold values from -0.0625 to 0.0625
- plan: int32 [64, 32], replicated, may hold values from 0 to 63, as said below
- lengths: int32 [8, 16], replicated, may hold values from 0 to 1024, as said below
Outputs:
- attended: bfloat16 [8192, 4096], P(('dp', 'ctx'), 'tensor')
- query_grad: bfloat16 [8192, 4096], P(('dp', 'ctx'), 'tensor')
- value_grad: bfloat16 [8192, 512], P(('dp', 'ctx'), 'tensor')
- feature_grad: bfloat16 [8192, 8192], P(('dp', 'ctx'), 'tensor')
- key_weight_grad: float32 [512, 8192], P(('dp', 'ctx'), 'tensor')
Inputs may be any that keep to these rules, and one draw needn't show every extreme that they name: `plan`: no row names a loader twice, and every loader is named exactly 32 times. `lengths`: each row sums to 1024; exactly one row is a single sequence of 1024 followed by zeros; every other row holds 16 sequences of 1 or more tokens.
All inputs are finite; a program needn't handle non-finite values.
Results may differ from a plain program's by a relative error of at most 0.035.
The roundings to bfloat16 on the way count: a program that leaves them out, or rounds other values in their place, can miss the bound.
Values may be sent and summed in bfloat16 or wider, within the bound.
A program may use at most 64 MiB of HBM per device.

v0:
```python
import math

import jax
import jax.numpy as jnp
from jax import lax
from jax.sharding import PartitionSpec as P

HEAD = 128


theta_base = 500000.0
masked_score = -1e30


def rotary_tables(offsets):
    half_dim = HEAD // 2
    exponent = jnp.arange(half_dim, dtype=jnp.float32) * (2.0 / HEAD)
    frequency = jnp.exp(-exponent * math.log(theta_base))
    angle = offsets.astype(jnp.float32)[:, None] * frequency[None, :]
    return (jnp.cos(angle), jnp.sin(angle))


def rotate(inputs, cosine, sine):
    half_dim = HEAD // 2
    first_half = inputs[..., :half_dim]
    second_half = inputs[..., half_dim:]
    return jnp.concatenate(
        [first_half * cosine - second_half * sine, second_half * cosine + first_half * sine],
        axis=-1,
    )


def unrotate(grads, cosine, sine):
    half_dim = HEAD // 2
    first_half = grads[..., :half_dim]
    second_half = grads[..., half_dim:]
    return jnp.concatenate(
        [first_half * cosine + second_half * sine, second_half * cosine - first_half * sine],
        axis=-1,
    )


def outgoing(array, chosen_slab, is_live, slab_count):
    blocks = array.reshape(slab_count, -1, array.shape[-1])
    picked = jnp.take(blocks, chosen_slab, axis=0)
    return jnp.where(is_live[:, None, None] > 0, picked, jnp.zeros_like(picked))


def arrange(received, chosen_slab):
    return jnp.take(received, chosen_slab, axis=0).reshape(-1, received.shape[-1])


def project_keys(features, key_weight):
    partial_keys = jnp.einsum("td,kd->tk", features, key_weight, preferred_element_type=jnp.float32)
    own_keys = lax.psum_scatter(partial_keys, "tensor", scatter_dimension=1, tiled=True)
    return lax.optimization_barrier(own_keys.astype(jnp.bfloat16))


def gather_heads(key_grad):
    return lax.all_gather(key_grad, "tensor", axis=1, tiled=True)


def weight_grads(all_grads, features):
    return lax.psum_scatter(
        jnp.einsum("tk,td->kd", all_grads, features, preferred_element_type=jnp.float32),
        ("dp", "ctx"),
        scatter_dimension=0,
        tiled=True,
    )


def shards(tokens, queries, values, out_grad, key_weight, plan, lengths):
    loaders = lax.axis_size(("dp", "ctx"))
    myself = lax.axis_index(("dp", "ctx"))
    group_index = lax.axis_index("dp")
    place_index = lax.axis_index("ctx")
    slab_count = plan.shape[1]
    local_rows = tokens.shape[0]
    heads_here = queries.shape[1] // HEAD
    loader_ids = jnp.arange(loaders, dtype=jnp.int32)
    slab_ids = jnp.arange(slab_count, dtype=jnp.int32)
    my_dests = lax.dynamic_index_in_dim(plan, myself, 0, keepdims=False)
    sends_to = (my_dests[None, :] == loader_ids[:, None]).astype(jnp.int32)
    send_live = jnp.sum(sends_to, axis=1)
    send_slab = jnp.sum(sends_to * slab_ids[None, :], axis=1)
    recv_live = jnp.sum((plan == myself).astype(jnp.int32), axis=1)
    recv_rank = jnp.cumsum(recv_live) - 1
    slot_match = ((recv_rank[:, None] == slab_ids[None, :]) & (recv_live[:, None] > 0)).astype(
        jnp.int32
    )
    from_loader = jnp.sum(slot_match * loader_ids[:, None], axis=0)
    back_slab = jnp.clip(recv_rank, 0, slab_count - 1)

    def send_out(array):
        return outgoing(array, send_slab, send_live, slab_count)

    moved = (
        lax.all_to_all(send_out(tokens), ("dp", "ctx"), split_axis=0, concat_axis=0, tiled=True),
        lax.all_to_all(send_out(queries), ("dp", "ctx"), split_axis=0, concat_axis=0, tiled=True),
        lax.all_to_all(send_out(values), ("dp", "ctx"), split_axis=0, concat_axis=0, tiled=True),
        lax.all_to_all(send_out(out_grad), ("dp", "ctx"), split_axis=0, concat_axis=0, tiled=True),
    )
    features = arrange(moved[0], from_loader)
    key_proj = project_keys(features, key_weight)
    query_ctx = arrange(moved[1], from_loader)
    value_ctx = arrange(moved[2], from_loader)
    grad_ctx = arrange(moved[3], from_loader)
    group_lengths = lax.dynamic_index_in_dim(lengths, group_index, 0, keepdims=False)
    group_ends = jnp.cumsum(group_lengths)
    position = place_index * local_rows + jnp.arange(local_rows, dtype=jnp.int32)
    seq_start = jnp.sum(
        group_lengths[None, :] * (group_ends[None, :] <= position[:, None]).astype(jnp.int32),
        axis=1,
    )
    cosine, sine = rotary_tables(position - seq_start)
    keys = rotate(key_proj.astype(jnp.float32), cosine, sine).astype(jnp.bfloat16)
    all_keys, all_values = (
        lax.all_gather(keys, "ctx", axis=0, tiled=True),
        lax.all_gather(value_ctx, "ctx", axis=0, tiled=True),
    )
    query_three = query_ctx.reshape(local_rows, heads_here, HEAD)
    grad_three = grad_ctx.reshape(local_rows, heads_here, HEAD)
    key_total = all_keys.shape[0]
    key_block = min(512, key_total)
    block_count = key_total // key_block
    block_offsets = jnp.arange(key_block, dtype=jnp.int32)
    scale = HEAD ** (-0.5)
    block_list = jnp.arange(block_count, dtype=jnp.int32)

    def block_scores(first_key):
        key_tile = lax.dynamic_slice_in_dim(all_keys, first_key, key_block, 0)
        scores = (
            jnp.einsum("qhd,kd->hqk", query_three, key_tile, preferred_element_type=jnp.float32)
            * scale
        )
        key_position = first_key + block_offsets
        visible = (key_position[None, :] <= position[:, None]) & (
            key_position[None, :] >= seq_start[:, None]
        )
        return (key_tile, scores, visible[None])

    def stat_step(carry, block_index):
        highest, summed = carry
        first_key = block_index * key_block
        key_tile, scores, visible = block_scores(first_key)
        new_high = jnp.maximum(highest, jnp.max(jnp.where(visible, scores, masked_score), axis=2))
        grown = jnp.sum(jnp.where(visible, jnp.exp(scores - new_high[..., None]), 0.0), axis=2)
        return ((new_high, summed * jnp.exp(highest - new_high) + grown), None)

    start_high = jnp.full((heads_here, local_rows), masked_score, jnp.float32)
    start_sum = jnp.zeros((heads_here, local_rows), jnp.float32)
    (highest, summed), _ = lax.scan(stat_step, (start_high, start_sum), block_list)
    log_total = highest + jnp.log(summed)

    def output_step(accum, block_index):
        first_key = block_index * key_block
        key_tile, scores, visible = block_scores(first_key)
        weights = jnp.where(visible, jnp.exp(scores - log_total[..., None]), 0.0).astype(
            jnp.bfloat16
        )
        value_tile = lax.dynamic_slice_in_dim(all_values, first_key, key_block, 0)
        return (
            accum
            + jnp.einsum("hqk,kd->qhd", weights, value_tile, preferred_element_type=jnp.float32),
            None,
        )

    out_accum, _ = lax.scan(
        output_step, jnp.zeros((local_rows, heads_here, HEAD), jnp.float32), block_list
    )
    attended = out_accum.astype(jnp.bfloat16)
    delta = jnp.sum(grad_three.astype(jnp.float32) * attended.astype(jnp.float32), axis=2).T

    def back_step(query_accum, block_index):
        first_key = block_index * key_block
        key_tile, scores, visible = block_scores(first_key)
        value_tile = lax.dynamic_slice_in_dim(all_values, first_key, key_block, 0)
        prob = jnp.where(visible, jnp.exp(scores - log_total[..., None]), 0.0)
        dprob = jnp.einsum(
            "qhd,kd->hqk", grad_three, value_tile, preferred_element_type=jnp.float32
        )
        dscore = (prob * (dprob - delta[..., None])).astype(jnp.bfloat16)
        new_accum = query_accum + jnp.einsum(
            "hqk,kd->qhd", dscore, key_tile, preferred_element_type=jnp.float32
        )
        key_term = (
            jnp.einsum("hqk,qhd->kd", dscore, query_three, preferred_element_type=jnp.float32)
            * scale
        )
        value_term = jnp.einsum(
            "hqk,qhd->kd", prob.astype(jnp.bfloat16), grad_three, preferred_element_type=jnp.float32
        )
        return (new_accum, jnp.concatenate([key_term, value_term], axis=1))

    query_accum, stacked = lax.scan(
        back_step, jnp.zeros((local_rows, heads_here, HEAD), jnp.float32), block_list
    )
    query_grad = (query_accum * scale).astype(jnp.bfloat16).reshape(local_rows, heads_here * HEAD)
    group_terms = stacked.reshape(key_total, 2 * HEAD)
    owned = lax.psum_scatter(
        group_terms.astype(jnp.bfloat16), "ctx", scatter_dimension=0, tiled=True
    ).astype(jnp.float32)
    key_grad = unrotate(owned[:, :HEAD], cosine, sine).astype(jnp.bfloat16)
    value_grad = owned[:, HEAD:].astype(jnp.bfloat16)
    all_grads = gather_heads(key_grad)
    context_grad = jnp.dot(all_grads, key_weight, preferred_element_type=jnp.float32).astype(
        jnp.bfloat16
    )
    returned = lax.all_to_all(
        outgoing(context_grad, back_slab, recv_live, slab_count),
        ("dp", "ctx"),
        split_axis=0,
        concat_axis=0,
        tiled=True,
    )
    feature_grad = arrange(returned, my_dests)
    key_weight_grad = weight_grads(all_grads, features)
    attended_flat = attended.reshape(local_rows, heads_here * HEAD)
    return (attended_flat, query_grad, value_grad, feature_grad, key_weight_grad)


def solution(mesh):
    placed = (
        P(("dp", "ctx"), "tensor"),
        P(("dp", "ctx"), "tensor"),
        P(("dp", "ctx"), "tensor"),
        P(("dp", "ctx"), "tensor"),
        P(None, "tensor"),
        P(),
        P(),
    )
    return jax.shard_map(
        shards,
        mesh=mesh,
        in_specs=placed,
        out_specs=(
            P(("dp", "ctx"), "tensor"),
            P(("dp", "ctx"), "tensor"),
            P(("dp", "ctx"), "tensor"),
            P(("dp", "ctx"), "tensor"),
            P(("dp", "ctx"), "tensor"),
        ),
        check_vma=False,
    )
```

profile of v0, /device:TPU:2, one launch (start us, length us, event | category | flops | bytes accessed | tf_op | source)
XLA Modules:
  0.0 576.1 jit_solution(2664606948630749765)
XLA Ops:
  7.2 1.0 dynamic-slice_reduce_fusion
  8.4 1.4 gather_fusion
  9.8 0.8 select_select_fusion.4
  10.6 13.1 %all-to-all-start = ((bf16[64,4,128]{2,1,0:T(4,128)(2,1)}), bf16[64,4,128]{2,1,0:T(4,128)(2,1)S(1)}, u32[]{:S(2)}, u32[]{:S(2)}) async-start(bf16[64,4,128]{2,1,0:T(4,128)(2,1)} %select_select_fusion.4), calls=%async_computation | async-start | bytes 131072 | tf_op jit(solution)/shard_map/all_to_all | solution.py:100
  23.8 1.2 reshape.352
  25.0 2.4 gather_fusion.2
  27.4 3.0 select_select_fusion.1
  30.4 3.1 all-to-all-done
  33.5 8.4 %all-to-all-start.1 = ((bf16[64,4,2048]{2,1,0:T(4,128)(2,1)}), bf16[64,4,2048]{2,1,0:T(4,128)(2,1)}, u32[]{:S(2)}, u32[]{:S(2)}) async-start(bf16[64,4,2048]{2,1,0:T(4,128)(2,1)} %select_select_fusion.1), calls=%async_computation.1 | async-start | bytes 2097152 | tf_op jit(solution)/shard_map/all_to_all | solution.py:98
  42.3 1.0 gather_fusion.4
  43.4 1.8 gather_fusion.6
  45.5 2.7 select_select_fusion.2
  48.2 21.1 %all-to-all-done.1 = bf16[64,4,2048]{2,1,0:T(4,128)(2,1)} async-done(((bf16[64,4,2048]{2,1,0:T(4,128)(2,1)}), bf16[64,4,2048]{2,1,0:T(4,128)(2,1)}, u32[]{:S(2)}, u32[]{:S(2)}) %all-to-all-start.1) | async-done | bytes 1048608 | tf_op jit(solution)/shard_map/all_to_all | solution.py:98
  69.3 7.0 %all-to-all-start.3 = ((bf16[64,4,1024]{2,1,0:T(4,128)(2,1)}), bf16[64,4,1024]{2,1,0:T(4,128)(2,1)}, u32[]{:S(2)}, u32[]{:S(2)}) async-start(bf16[64,4,1024]{2,1,0:T(4,128)(2,1)} %get-tuple-element.535), calls=%async_computation.4 | async-start | bytes 1048576 | tf_op jit(solution)/shard_map/all_to_all | solution.py:101
  76.3 0.7 fusion.78
  77.6 0.6 gather_fusion.1
  78.2 2.2 gather_fusion.3
  80.4 12.6 %all-to-all-done.3 = bf16[64,4,1024]{2,1,0:T(4,128)(2,1)} async-done(((bf16[64,4,1024]{2,1,0:T(4,128)(2,1)}), bf16[64,4,1024]{2,1,0:T(4,128)(2,1)}, u32[]{:S(2)}, u32[]{:S(2)}) %all-to-all-start.3) | async-done | bytes 524320 | tf_op jit(solution)/shard_map/all_to_all | solution.py:101
  93.0 5.8 %all-to-all-start.2 = ((bf16[64,4,1024]{2,1,0:T(4,128)(2,1)}), bf16[64,4,1024]{2,1,0:T(4,128)(2,1)}, u32[]{:S(2)}, u32[]{:S(2)}) async-start(bf16[64,4,1024]{2,1,0:T(4,128)(2,1)} %get-tuple-element.536), calls=%async_computation.3 | async-start | bytes 1048576 | tf_op jit(solution)/shard_map/all_to_all | solution.py:99
  98.9 1.1 broadcast_select_fusion.1
  100.0 1.2 reshape.353
  101.2 1.4 fusion.79
  102.8 30.9 %all_gather.9 = bf16[1024,128]{1,0:T(8,128)(2,1)} all-gather(bf16[128,128]{1,0:T(8,128)(2,1)S(1)} %broadcast_select_fusion.4), channel_id=1, replica_groups=mesh['dp'=8,'ctx'=8,'tensor'=4] {'ctx'}, dimensions={0}, use_global_device_ids=true | all-gather | bytes 294912 | tf_op jit(solution)/shard_map/all_gather | solution.py:119
  133.7 1.8 gather_fusion.7
  135.5 2.5 gather_fusion.5
  138.0 2.0 broadcast_select_fusion.2
  140.0 1.1 reshape_reshape.6
  141.1 0.7 copy.114
  142.1 1.1 reshape_reshape.7
  143.4 0.8 convert_element_type.59
  144.5 25.7 %all_gather.10 = bf16[1024,128]{0,1:T(8,128)(2,1)} all-gather(bf16[128,128]{0,1:T(8,128)(2,1)S(1)} %pad_maximum_fusion), channel_id=1, replica_groups=mesh['dp'=8,'ctx'=8,'tensor'=4] {'ctx'}, dimensions={0}, use_global_device_ids=true | all-gather | bytes 294912 | tf_op jit(solution)/shard_map/all_gather | solution.py:118
  170.2 1.1 copy.113
  171.4 6.7 %while.37 = (s32[]{:T(128)}, f32[8,128]{1,0:T(8,128)S(1)}, f32[8,128]{1,0:T(8,128)S(1)}, s32[2]{0:T(128)S(1)}, s32[128]{0:T(128)S(1)}, /*index=5*/bf16[1024,128]...) while((s32[]{:T(128)}, f32[8,128]{1,0:T(8,128)S(1)}, ...), condition=%wide.region_11.16_spmd.clone, body=%wide.region_8.15_spmd.clone.sunk | while | flops 138090112 | bytes 4843214 | solution.py:152
  171.4 0.6 dynamic_slice.86
  172.8 1.4 fusion.119
  174.7 0.6 dynamic_slice.86
  176.1 1.4 fusion.119
  178.1 8.0 %while.38 = (s32[]{:T(128)}, f32[128,8,128]{0,2,1:T(8,128)}, s32[2]{0:T(128)S(1)}, bf16[1024,128]{1,0:T(8,128)(2,1)}, s32[128]{0:T(128)S(1)}, /*index=5*/bf16[10...) while((s32[]{:T(128)}, f32[128,8,128]{0,2,1:T(8,128)}, ...), condition=%wide.region_13.18_spmd.clone, body=%wide.region_12.17_spmd.clone.sunk | while | flops 270992000 | bytes 1715408 | solution.py:168
  178.1 0.6 dynamic_slice.89
  179.5 2.5 fusion.125
  183.4 2.7 fusion.125
  186.1 2.0 copy.115
  188.1 1.2 multiply_reduce_fusion
  189.4 9.6 %while.39 = (s32[]{:T(128)}, f32[128,8,128]{0,2,1:T(8,128)S(1)}, bf16[2,512,256]{1,2,0:T(8,128)(2,1)}, s32[2]{0:T(128)S(1)}, bf16[1024,128]{1,0:T(8,128)(2,1)S(1...) while((s32[]{:T(128)}, f32[128,8,128]{0,2,1:T(8,128)S(1)}, ...), condition=%wide.region_16.21_spmd.clone, body=%wide.region_15.20_spmd.clone.sunk | while | flops 675873408 | bytes 18102092 | solution.py:195
  189.4 0.6 dynamic_slice.93
  193.4 0.8 copy-done.7
  198.1 0.8 copy-done.7
  199.0 2.1 copy.135
  201.1 39.6 %reduce-scatter.10.cloned.1.call-done = bf16[128,256]{1,0:T(8,128)(2,1)} async-done(((bf16[1024,256]{1,0:T(8,128)(2,1)}), bf16[128,256]{1,0:T(8,128)(2,1)}) %reduce-scatter.10.cloned.1.call-update) | async-done | bytes 65552
  240.8 0.9 copy.134
  241.9 6.9 %all_gather.11 = bf16[128,512]{0,1:T(8,128)(2,1)S(1)} all-gather(bf16[128,128]{0,1:T(8,128)(2,1)S(1)} %pad_maximum_fusion.1), channel_id=1, replica_groups=mesh['dp'=8,'ctx'=8,'tensor'=4] {'tensor'}, dimensions={1}, use_global_device_ids=true | all-gather | bytes 163840 | tf_op jit(solution)/shard_map/all_gather | solution.py:60
  248.9 2.6 fusion.80
  251.6 1.3 convolution_convert_fusion
  252.8 1.2 reshape.358
  254.1 2.4 gather_fusion.8
  256.5 3.0 select_select_fusion
  259.4 10.1 %all-to-all-start.4 = ((bf16[64,4,2048]{2,1,0:T(4,128)(2,1)}), bf16[64,4,2048]{2,1,0:T(4,128)(2,1)}, u32[]{:S(2)}, u32[]{:S(2)}) async-start(bf16[64,4,2048]{2,1,0:T(4,128)(2,1)} %select_select_fusion), calls=%async_computation.5 | async-start | bytes 2097152 | tf_op jit(solution)/shard_map/all_to_all | solution.py:209
  269.6 0.8 copy.140
  270.4 0.9 copy.131
  271.3 0.7 copy.122
  272.0 25.9 %all-to-all-done.4 = bf16[64,4,2048]{2,1,0:T(4,128)(2,1)} async-done(((bf16[64,4,2048]{2,1,0:T(4,128)(2,1)}), bf16[64,4,2048]{2,1,0:T(4,128)(2,1)}, u32[]{:S(2)}, u32[]{:S(2)}) %all-to-all-start.4) | async-done | bytes 1048608 | tf_op jit(solution)/shard_map/all_to_all | solution.py:209
  297.9 2.2 gather_fusion.9
  300.5 0.9 reshape.359
  301.4 268.2 %reduce-scatter.8.cloned.1.call-done = f32[8,2048]{1,0:T(8,128)} async-done(((f32[512,2048]{1,0:T(8,128)}), f32[8,2048]{1,0:T(8,128)}) %reduce-scatter.8.cloned.1.call-update) | async-done | bytes 65552 | tf_op jit(solution)/shard_map/reduce_scatter | solution.py:64
  (129 shorter events, 10.9 us)
Async XLA Ops:
  7.2 94.0 %copy-start = (bf16[512,2048]{1,0:T(8,128)(2,1)S(1)}, bf16[512,2048]{1,0:T(8,128)(2,1)}, u32[]{:S(2)}) copy-start(bf16[512,2048]{1,0:T(8,128)(2,1)} %param.25) | copy-start | bytes 6291460
  10.6 22.9 %all-to-all-start = ((bf16[64,4,128]{2,1,0:T(4,128)(2,1)}), bf16[64,4,128]{2,1,0:T(4,128)(2,1)S(1)}, u32[]{:S(2)}, u32[]{:S(2)}) async-start(bf16[64,4,128]{2,1,0:T(4,128)(2,1)} %select_select_fusion.4), calls=%async_computation | async-start | bytes 131072 | tf_op jit(solution)/shard_map/all_to_all | solution.py:100
  27.4 14.6 %copy-start.10 = (s32[64,32]{0,1:T(8,128)S(1)}, s32[64,32]{0,1:T(8,128)}, u32[]{:S(2)}) copy-start(s32[64,32]{0,1:T(8,128)} %param.26) | copy-start | bytes 24580
  27.4 14.8 %copy-start.8 = (bf16[128,1024]{1,0:T(8,128)(2,1)S(1)}, bf16[128,1024]{1,0:T(8,128)(2,1)}, u32[]{:S(2)}) copy-start(bf16[128,1024]{1,0:T(8,128)(2,1)} %param.22) | copy-start | bytes 786436
  30.4 12.9 %copy-start.9 = (bf16[128,1024]{1,0:T(8,128)(2,1)S(1)}, bf16[128,1024]{1,0:T(8,128)(2,1)}, u32[]{:S(2)}) copy-start(bf16[128,1024]{1,0:T(8,128)(2,1)} %param.24) | copy-start | bytes 786436
  33.5 35.7 %all-to-all-start.1 = ((bf16[64,4,2048]{2,1,0:T(4,128)(2,1)}), bf16[64,4,2048]{2,1,0:T(4,128)(2,1)}, u32[]{:S(2)}, u32[]{:S(2)}) async-start(bf16[64,4,2048]{2,1,0:T(4,128)(2,1)} %select_select_fusion.1), calls=%async_computation.1 | async-start | bytes 2097152 | tf_op jit(solution)/shard_map/all_to_all | solution.py:98
  69.3 23.7 %all-to-all-start.3 = ((bf16[64,4,1024]{2,1,0:T(4,128)(2,1)}), bf16[64,4,1024]{2,1,0:T(4,128)(2,1)}, u32[]{:S(2)}, u32[]{:S(2)}) async-start(bf16[64,4,1024]{2,1,0:T(4,128)(2,1)} %get-tuple-element.535), calls=%async_computation.4 | async-start | bytes 1048576 | tf_op jit(solution)/shard_map/all_to_all | solution.py:101
  93.0 42.5 %all-to-all-start.2 = ((bf16[64,4,1024]{2,1,0:T(4,128)(2,1)}), bf16[64,4,1024]{2,1,0:T(4,128)(2,1)}, u32[]{:S(2)}, u32[]{:S(2)}) async-start(bf16[64,4,1024]{2,1,0:T(4,128)(2,1)} %get-tuple-element.536), calls=%async_computation.3 | async-start | bytes 1048576 | tf_op jit(solution)/shard_map/all_to_all | solution.py:99
  98.8 44.6 %reduce-scatter.6.cloned.1.call-start = ((), (), s32[]{:S(2)}) async-start(), calls=%async_computation.8 | async-start | bytes 327680 | tf_op jit(solution)/shard_map/reduce_scatter | solution.py:55
  101.2 36.8 %copy-start.1 = (bf16[128,2048]{1,0:T(8,128)(2,1)}, bf16[128,2048]{1,0:T(8,128)(2,1)S(1)}, u32[]{:S(2)}) copy-start(bf16[128,2048]{1,0:T(8,128)(2,1)S(1)} %reshape.353) | copy-start | bytes 1572868
  102.6 138.1 %reduce-scatter.10.cloned.1.call-start = ((), (), s32[]{:S(2)}) async-start(), calls=%async_computation.10 | async-start | bytes 589824
  143.1 1.4 copy-start.5
  190.8 1.1 copy-start.3
  192.3 1.0 copy-start.6
  193.4 0.8 copy-start.7
  195.6 1.1 copy-start.3
  197.1 1.0 copy-start.6
  198.1 0.8 copy-start.7
  199.0 49.9 %copy-start.2 = (bf16[128,2048]{1,0:T(8,128)(2,1)S(1)}, bf16[128,2048]{1,0:T(8,128)(2,1)}, u32[]{:S(2)}) copy-start(bf16[128,2048]{1,0:T(8,128)(2,1)} %copy-done.1) | copy-start | bytes 1572868
  201.1 368.5 %reduce-scatter.8.cloned.1.call-start = ((), (), s32[]{:S(2)}) async-start(), calls=%async_computation.9 | async-start | bytes 4259840 | tf_op jit(solution)/shard_map/reduce_scatter | solution.py:64
  256.5 13.1 %copy-start.4 = (bf16[128,8,128]{2,1,0:T(8,128)(2,1)S(1)}, bf16[128,8,128]{2,1,0:T(8,128)(2,1)}, u32[]{:S(2)}) copy-start(bf16[128,8,128]{2,1,0:T(8,128)(2,1)} %copy.115) | copy-start | bytes 786436
  259.4 38.5 %all-to-all-start.4 = ((bf16[64,4,2048]{2,1,0:T(4,128)(2,1)}), bf16[64,4,2048]{2,1,0:T(4,128)(2,1)}, u32[]{:S(2)}, u32[]{:S(2)}) async-start(bf16[64,4,2048]{2,1,0:T(4,128)(2,1)} %select_select_fusion), calls=%async_computation.5 | async-start | bytes 2097152 | tf_op jit(solution)/shard_map/all_to_all | solution.py:209
Sparse Core Ops, SparseCore 0:
  103.0 32.0 reduce-scatter.5
  201.2 39.5 reduce-scatter.9
  251.6 317.8 reduce-scatter.7
where the time goes:
time: 586 us; the launch traced here: 576 us
  waiting for transfers between devices  371 us (63%)
  blocking collectives  63.6 us (11%)
  starting transfers between devices  44.6 us (8%)
  local copies, waits for them, and re-layouts  42.5 us (7%)
  other arithmetic  18.3 us (3%)
  matrix products  18 us (3%)
  between operations  14.2 us (2%)
    reduce_scatter x1, waiting for transfers between devices, weight_grads(): lax.psum_scatter(jnp.einsum('tk,td->kd', all_grads, features, preferred_e...  268 us
    unnamed x4, waiting for transfers between devices  39.7 us
    all_gather x1, blocking collectives, shards(): lax.all_gather(value_ctx, 'ctx', axis=0, tiled=True)  30.9 us
    all_to_all x1, waiting for transfers between devices, shards(): lax.all_to_all(outgoing(context_grad, back_slab, recv_live, slab_count),...  25.9 us
    all_gather x1, blocking collectives, shards(): lax.all_gather(keys, 'ctx', axis=0, tiled=True)  25.7 us
    all_to_all x1, waiting for transfers between devices, shards(): lax.all_to_all(send_out(tokens), ('dp', 'ctx'), split_axis=0, concat_axis...  21.1 us
    all_to_all x1, starting transfers between devices, shards(): lax.all_to_all(send_out(values), ('dp', 'ctx'), split_axis=0, concat_axis...  13.1 us
    all_to_all x1, waiting for transfers between devices, shards(): lax.all_to_all(send_out(out_grad), ('dp', 'ctx'), split_axis=0, concat_ax...  12.6 us
  transfers between devices with their start and end apart: 8, of which 6 were waited for; matrix products, arithmetic and copies ran while one was open for 8% of the time, Pallas kernels for 0%

commit v1 on v0

--- a/solution.py
+++ b/solution.py
@@ -61,12 +61,12 @@
 
 
 def weight_grads(all_grads, features):
-    return lax.psum_scatter(
-        jnp.einsum("tk,td->kd", all_grads, features, preferred_element_type=jnp.float32),
-        ("dp", "ctx"),
-        scatter_dimension=0,
-        tiled=True,
-    )
+    terms = jnp.einsum("tk,td->kd", all_grads, features, preferred_element_type=jnp.float32)
+    moved = lax.all_to_all(
+        terms.astype(jnp.bfloat16), ("dp", "ctx"), split_axis=0, concat_axis=0, tiled=True
+    )
+    parts = moved.reshape(lax.axis_size(("dp", "ctx")), -1, moved.shape[-1])
+    return jnp.sum(parts.astype(jnp.float32), axis=0)
 
 
 def shards(tokens, queries, values, out_grad, key_weight, plan, lengths):
@@ -94,17 +94,15 @@
     def send_out(array):
         return outgoing(array, send_slab, send_live, slab_count)
 
-    moved = (
-        lax.all_to_all(send_out(tokens), ("dp", "ctx"), split_axis=0, concat_axis=0, tiled=True),
-        lax.all_to_all(send_out(queries), ("dp", "ctx"), split_axis=0, concat_axis=0, tiled=True),
-        lax.all_to_all(send_out(values), ("dp", "ctx"), split_axis=0, concat_axis=0, tiled=True),
-        lax.all_to_all(send_out(out_grad), ("dp", "ctx"), split_axis=0, concat_axis=0, tiled=True),
-    )
-    features = arrange(moved[0], from_loader)
-    key_proj = project_keys(features, key_weight)
-    query_ctx = arrange(moved[1], from_loader)
-    value_ctx = arrange(moved[2], from_loader)
-    grad_ctx = arrange(moved[3], from_loader)
+    raw_key = project_keys(tokens, key_weight)
+    grouped = jnp.concatenate([queries, out_grad, values, raw_key], axis=1)
+    moved = lax.all_to_all(send_out(grouped), ("dp", "ctx"), split_axis=0, concat_axis=0, tiled=True)
+    arranged = arrange(moved, from_loader)
+    width = queries.shape[1]
+    query_ctx = arranged[:, :width]
+    grad_ctx = arranged[:, width : 2 * width]
+    value_ctx = arranged[:, 2 * width : 2 * width + HEAD]
+    key_proj = arranged[:, 2 * width + HEAD :]
     group_lengths = lax.dynamic_index_in_dim(lengths, group_index, 0, keepdims=False)
     group_ends = jnp.cumsum(group_lengths)
     position = place_index * local_rows + jnp.arange(local_rows, dtype=jnp.int32)
@@ -114,10 +112,8 @@
     )
     cosine, sine = rotary_tables(position - seq_start)
     keys = rotate(key_proj.astype(jnp.float32), cosine, sine).astype(jnp.bfloat16)
-    all_keys, all_values = (
-        lax.all_gather(keys, "ctx", axis=0, tiled=True),
-        lax.all_gather(value_ctx, "ctx", axis=0, tiled=True),
-    )
+    both = lax.all_gather(jnp.concatenate([keys, value_ctx], axis=1), "ctx", axis=0, tiled=True)
+    all_keys, all_values = both[:, :HEAD], both[:, HEAD:]
     query_three = query_ctx.reshape(local_rows, heads_here, HEAD)
     grad_three = grad_ctx.reshape(local_rows, heads_here, HEAD)
     key_total = all_keys.shape[0]
@@ -202,19 +198,18 @@
     ).astype(jnp.float32)
     key_grad = unrotate(owned[:, :HEAD], cosine, sine).astype(jnp.bfloat16)
     value_grad = owned[:, HEAD:].astype(jnp.bfloat16)
-    all_grads = gather_heads(key_grad)
-    context_grad = jnp.dot(all_grads, key_weight, preferred_element_type=jnp.float32).astype(
-        jnp.bfloat16
-    )
     returned = lax.all_to_all(
-        outgoing(context_grad, back_slab, recv_live, slab_count),
+        outgoing(key_grad, back_slab, recv_live, slab_count),
         ("dp", "ctx"),
         split_axis=0,
         concat_axis=0,
         tiled=True,
     )
-    feature_grad = arrange(returned, my_dests)
-    key_weight_grad = weight_grads(all_grads, features)
+    all_grads = gather_heads(arrange(returned, my_dests))
+    feature_grad = jnp.dot(all_grads, key_weight, preferred_element_type=jnp.float32).astype(
+        jnp.bfloat16
+    )
+    key_weight_grad = weight_grads(all_grads, tokens)
     attended_flat = attended.reshape(local_rows, heads_here * HEAD)
     return (attended_flat, query_grad, value_grad, feature_grad, key_weight_grad)
 

time: 586 us -> 299 us (0.51); the launches traced: 576 us -> 298 us
  waiting for transfers between devices: 371 us -> 155 us
  blocking collectives: 63.6 us -> 36 us
  local copies, waits for them, and re-layouts: 42.5 us -> 25.5 us
  starting transfers between devices: 44.6 us -> 28 us
    reduce_scatter x1, waiting for transfers between devices: 268 us -> 35.4 us  [shards(): lax.psum_scatter(group_terms.astype(jnp.bfloat16), 'ctx', scatter_dimensi...]
    unnamed x4 -> x2, waiting for transfers between devices: 39.7 us -> 0.03 us
    reduce_scatter x1, waiting for transfers between devices: 0.02 us -> 33.4 us  [project_keys(): lax.psum_scatter(partial_keys, 'tensor', scatter_dimension=1, tiled=True)]
    all_gather x2 -> x1, blocking collectives: 56.6 us -> 29.1 us  [shards(): lax.all_gather(jnp.concatenate([keys, value_ctx], axis=1), 'ctx', axis=0,...]
    all_to_all x5 -> x3, waiting for transfers between devices: 62.7 us -> 86.3 us  [the longest x1 47.6 us: weight_grads(): lax.all_to_all(terms.astype(jnp.bfloat16), ('dp', 'ctx'), split_axis=0, c...]
    all_to_all x5 -> x3, starting transfers between devices: 44.5 us -> 27.9 us  [the longest x1 11.7 us: shards(): lax.all_to_all(send_out(grouped), ('dp', 'ctx'), split_axis=0, concat_axi...]
  transfers between devices with their start and end apart: 8 -> 5, of which waited for: 6 -> 5; matrix products, arithmetic and copies ran while one was open for 8% -> 2% of each run, Pallas kernels for 0% -> 0%
where the time goes in v1:
time: 299 us; the launch traced here: 298 us
  waiting for transfers between devices  155 us (52%)
  blocking collectives  36 us (12%)
  starting transfers between devices  28 us (9%)
  local copies, waits for them, and re-layouts  25.5 us (9%)
  matrix products  18.5 us (6%)
  other arithmetic  15.7 us (5%)
  between operations  14.4 us (5%)
  loops' own time  4.5 us (2%)
    all_to_all x1, waiting for transfers between devices, weight_grads(): lax.all_to_all(terms.astype(jnp.bfloat16), ('dp', 'ctx'), split_axis=0, c...  47.6 us
    reduce_scatter x1, waiting for transfers between devices, shards(): lax.psum_scatter(group_terms.astype(jnp.bfloat16), 'ctx', scatter_dimensi...  35.4 us
    reduce_scatter x1, waiting for transfers between devices, project_keys(): lax.psum_scatter(partial_keys, 'tensor', scatter_dimension=1, tiled=True)  33.4 us
    all_to_all x1, waiting for transfers between devices, shards(): lax.all_to_all(send_out(grouped), ('dp', 'ctx'), split_axis=0, concat_axi...  29.1 us
    all_gather x1, blocking collectives, shards(): lax.all_gather(jnp.concatenate([keys, value_ctx], axis=1), 'ctx', axis=0,...  29.1 us
    all_to_all x1, starting transfers between devices, shards(): lax.all_to_all(send_out(grouped), ('dp', 'ctx'), split_axis=0, concat_axi...  11.7 us
    all_to_all x1, starting transfers between devices, shards(): lax.all_to_all(outgoing(key_grad, back_slab, recv_live, slab_count), ('dp...  9.97 us
    all_to_all x1, waiting for transfers between devices, shards(): lax.all_to_all(outgoing(key_grad, back_slab, recv_live, slab_count), ('dp...  9.58 us
  transfers between devices with their start and end apart: 5, of which 5 were waited for; matrix products, arithmetic and copies ran while one was open for 2% of the time, Pallas kernels for 0%

profile of v1, /device:TPU:2, one launch (start us, length us, event | category | flops | bytes accessed | tf_op | source)
XLA Modules:
  0.0 297.8 jit_solution(7188971370558773540)
XLA Ops:
  7.3 1.5 copy-done
  8.8 2.6 fusion.83
  12.3 33.4 %reduce-scatter.3.cloned.1.call-done = f32[128,128]{1,0:T(8,128)} async-done(((f32[128,512]{1,0:T(8,128)}), f32[128,128]{1,0:T(8,128)}) %reduce-scatter.3.cloned.1.call-update) | async-done | bytes 65552 | tf_op jit(solution)/shard_map/reduce_scatter | solution.py:55
  45.7 0.8 convert_element_type.66
  46.5 0.9 pad_maximum_fusion
  47.4 1.5 reshape.374
  48.9 2.5 gather_fusion
  51.5 3.1 %select_select_fusion = bf16[64,4,2304]{2,1,0:T(4,128)(2,1)} fusion(bf16[64,4,2304]{2,1,0:T(4,128)(2,1)} %gather_fusion, pred[64]{0:T(512)(128)(4,1)S(1)} %get-tuple-element.456, pred[64]{0:T(512)(128)(4,1)S(1)} %get-tuple-element.457), kind=kLoop, calls=%fused_computation.77 | loop fusion | flops 1179648 | bytes 2359424 | tf_op jit(solution)/shard_map/jit(_where)/select_n | solution.py:46
  54.6 11.7 %all-to-all-start = ((bf16[64,4,2304]{2,1,0:T(4,128)(2,1)}), bf16[64,4,2304]{2,1,0:T(4,128)(2,1)}, u32[]{:S(2)}, u32[]{:S(2)}) async-start(bf16[64,4,2304]{2,1,0:T(4,128)(2,1)} %select_select_fusion), calls=%async_computation.1 | async-start | bytes 2359296 | tf_op jit(solution)/shard_map/all_to_all | solution.py:99
  66.3 0.7 fusion.81
  67.7 29.1 %all-to-all-done = bf16[64,4,2304]{2,1,0:T(4,128)(2,1)} async-done(((bf16[64,4,2304]{2,1,0:T(4,128)(2,1)}), bf16[64,4,2304]{2,1,0:T(4,128)(2,1)}, u32[]{:S(2)}, u32[]{:S(2)}) %all-to-all-start) | async-done | bytes 1179680 | tf_op jit(solution)/shard_map/all_to_all | solution.py:99
  96.9 2.3 gather_fusion.1
  99.2 0.9 gather.22
  100.1 1.2 broadcast_select_fusion
  101.3 0.8 slice_bitcast_fusion.1
  102.4 1.1 copy.81
  103.6 0.8 copy.86
  104.7 29.1 %all_gather.6 = bf16[1024,256]{1,0:T(8,128)(2,1)S(1)} all-gather(bf16[128,256]{1,0:T(8,128)(2,1)S(1)} %pad_maximum_fusion.1), channel_id=1, replica_groups=mesh['dp'=8,'ctx'=8,'tensor'=4] {'ctx'}, dimensions={0}, use_global_device_ids=true | all-gather | bytes 589824 | tf_op jit(solution)/shard_map/all_gather | solution.py:115
  133.8 0.7 fusion.82
  134.6 6.9 %while.37 = (s32[]{:T(128)}, f32[8,128]{1,0:T(8,128)S(1)}, f32[8,128]{1,0:T(8,128)S(1)}, s32[2]{0:T(128)S(1)}, s32[128]{0:T(128)S(1)}, /*index=5*/bf16[1024,128]...) while((s32[]{:T(128)}, f32[8,128]{1,0:T(8,128)S(1)}, ...), condition=%wide.region_11.12_spmd.clone, body=%wide.region_8.11_spmd.clone.sunk | while | flops 138090112 | bytes 4843214 | solution.py:148
  134.6 0.7 dynamic_slice.86
  136.1 1.4 fusion.122
  137.5 0.4 fusion.123
  138.0 0.7 dynamic_slice.86
  139.6 1.4 fusion.122
  141.0 0.4 fusion.123
  141.5 8.3 %while.38 = (s32[]{:T(128)}, f32[128,8,128]{0,2,1:T(8,128)}, s32[2]{0:T(128)S(1)}, bf16[1024,128]{1,0:T(8,128)(2,1)}, s32[128]{0:T(128)S(1)}, /*index=5*/bf16[10...) while((s32[]{:T(128)}, f32[128,8,128]{0,2,1:T(8,128)}, ...), condition=%wide.region_13.14_spmd.clone, body=%wide.region_12.13_spmd.clone.sunk | while | flops 270992000 | bytes 1715408 | solution.py:164
  141.5 0.7 dynamic_slice.89
  143.0 2.5 fusion.128
  145.6 0.7 dynamic_slice.89
  147.1 2.7 fusion.128
  149.8 1.8 multiply_reduce_fusion
  151.6 9.6 %while.39 = (s32[]{:T(128)}, f32[128,8,128]{0,2,1:T(8,128)S(1)}, bf16[2,512,256]{1,2,0:T(8,128)(2,1)}, s32[2]{0:T(128)S(1)}, bf16[1024,128]{1,0:T(8,128)(2,1)S(1...) while((s32[]{:T(128)}, f32[128,8,128]{0,2,1:T(8,128)S(1)}, ...), condition=%wide.region_16.17_spmd.clone, body=%wide.region_15.16_spmd.clone.sunk | while | flops 675873408 | bytes 18102092 | solution.py:191
  151.6 0.6 dynamic_slice.93
  153.0 0.6 fusion.139
  153.6 0.5 convolution_bitcast_fusion.4
  154.1 0.4 fusion.140
  154.5 0.5 fusion.142
  155.0 0.4 fusion.141
  155.6 0.8 copy-done.5
  156.4 0.6 dynamic_slice.93
  157.8 0.6 fusion.139
  158.3 0.5 convolution_bitcast_fusion.4
  158.8 0.4 fusion.140
  159.3 0.5 fusion.142
  159.8 0.4 fusion.141
  160.3 0.8 copy-done.5
  161.1 2.1 copy.70
  163.3 35.4 %reduce-scatter.5.cloned.1.call-done = bf16[128,256]{1,0:T(8,128)(2,1)} async-done(((bf16[1024,256]{1,0:T(8,128)(2,1)}), bf16[128,256]{1,0:T(8,128)(2,1)}) %reduce-scatter.5.cloned.1.call-update) | async-done | bytes 65552 | tf_op jit(solution)/shard_map/reduce_scatter | solution.py:196
  198.7 0.8 convert_element_type.75
  199.9 0.7 gather_fusion.2
  200.6 0.8 select_select_fusion.1
  201.4 10.0 %all-to-all-start.1 = ((bf16[64,4,128]{2,1,0:T(4,128)(2,1)}), bf16[64,4,128]{2,1,0:T(4,128)(2,1)S(1)}, u32[]{:S(2)}, u32[]{:S(2)}) async-start(bf16[64,4,128]{2,1,0:T(4,128)(2,1)} %select_select_fusion.1), calls=%async_computation.3 | async-start | bytes 131072 | tf_op jit(solution)/shard_map/all_to_all | solution.py:201
  211.6 9.6 %all-to-all-done.1 = bf16[64,4,128]{2,1,0:T(4,128)(2,1)S(1)} async-done(((bf16[64,4,128]{2,1,0:T(4,128)(2,1)}), bf16[64,4,128]{2,1,0:T(4,128)(2,1)S(1)}, u32[]{:S(2)}, u32[]{:S(2)}) %all-to-all-start.1) | async-done | bytes 65568 | tf_op jit(solution)/shard_map/all_to_all | solution.py:201
  221.2 0.6 gather_fusion.3
  221.9 7.0 %all_gather.7 = bf16[128,512]{1,0:T(8,128)(2,1)S(1)} all-gather(bf16[128,128]{1,0:T(8,128)(2,1)S(1)} %broadcast_select_fusion.1), channel_id=1, replica_groups=mesh['dp'=8,'ctx'=8,'tensor'=4] {'tensor'}, dimensions={1}, use_global_device_ids=true | all-gather | bytes 163840 | tf_op jit(solution)/shard_map/all_gather | solution.py:60
  228.9 2.0 fusion.58
  230.9 6.3 %all-to-all-start.2 = ((bf16[64,8,2048]{2,1,0:T(8,128)(2,1)}), bf16[64,8,2048]{2,1,0:T(8,128)(2,1)}, u32[]{:S(2)}, u32[]{:S(2)}) async-start(bf16[64,8,2048]{2,1,0:T(8,128)(2,1)} %fusion.58), calls=%async_computation.4 | async-start | bytes 4194304 | tf_op jit(solution)/shard_map/all_to_all | solution.py:65
  237.2 0.9 copy.78
  238.1 0.9 copy.79
  239.0 0.6 slice.64
  239.6 1.2 convolution_convert_fusion.1
  240.8 47.6 %all-to-all-done.2 = bf16[64,8,2048]{2,1,0:T(8,128)(2,1)} async-done(((bf16[64,8,2048]{2,1,0:T(8,128)(2,1)}), bf16[64,8,2048]{2,1,0:T(8,128)(2,1)}, u32[]{:S(2)}, u32[]{:S(2)}) %all-to-all-start.2) | async-done | bytes 2097184 | tf_op jit(solution)/shard_map/all_to_all | solution.py:65
  288.4 2.5 convert_reduce_fusion
  (103 shorter events, 4.4 us)
Async XLA Ops:
  7.2 1.6 copy-start
  7.2 4.2 %copy-start.9 = (s32[64,32]{0,1:T(8,128)S(1)}, s32[64,32]{0,1:T(8,128)}, u32[]{:S(2)}) copy-start(s32[64,32]{0,1:T(8,128)} %param.18) | copy-start | bytes 24580
  7.2 39.3 %copy-start.6 = (bf16[128,1024]{1,0:T(8,128)(2,1)S(1)}, bf16[128,1024]{1,0:T(8,128)(2,1)}, u32[]{:S(2)}) copy-start(bf16[128,1024]{1,0:T(8,128)(2,1)} %param.16) | copy-start | bytes 786436
  7.2 39.3 %copy-start.10 = (bf16[128,128]{1,0:T(8,128)(2,1)S(1)}, bf16[128,128]{1,0:T(8,128)(2,1)}, u32[]{:S(2)}) copy-start(bf16[128,128]{1,0:T(8,128)(2,1)} %param.15) | copy-start | bytes 98308
  7.2 39.3 %copy-start.7 = (bf16[128,1024]{1,0:T(8,128)(2,1)S(1)}, bf16[128,1024]{1,0:T(8,128)(2,1)}, u32[]{:S(2)}) copy-start(bf16[128,1024]{1,0:T(8,128)(2,1)} %param.14) | copy-start | bytes 786436
  7.2 38.5 %reduce-scatter.3.cloned.1.call-start = ((), (), s32[]{:S(2)}) async-start(), calls=%async_computation.5 | async-start | bytes 327680 | tf_op jit(solution)/shard_map/reduce_scatter | solution.py:55
  54.6 42.3 %all-to-all-start = ((bf16[64,4,2304]{2,1,0:T(4,128)(2,1)}), bf16[64,4,2304]{2,1,0:T(4,128)(2,1)}, u32[]{:S(2)}, u32[]{:S(2)}) async-start(bf16[64,4,2304]{2,1,0:T(4,128)(2,1)} %select_select_fusion), calls=%async_computation.1 | async-start | bytes 2359296 | tf_op jit(solution)/shard_map/all_to_all | solution.py:99
  66.2 132.4 %reduce-scatter.5.cloned.1.call-start = ((), (), s32[]{:S(2)}) async-start(), calls=%async_computation.6 | async-start | bytes 589824 | tf_op jit(solution)/shard_map/reduce_scatter | solution.py:196
  153.0 1.1 copy-start.1
  154.5 1.0 copy-start.4
  155.6 0.8 copy-start.5
  157.8 1.1 copy-start.1
  159.3 1.0 copy-start.4
  160.3 0.8 copy-start.5
  161.1 67.7 %copy-start.2 = (bf16[128,2048]{1,0:T(8,128)(2,1)S(1)}, bf16[128,2048]{1,0:T(8,128)(2,1)}, u32[]{:S(2)}) copy-start(bf16[128,2048]{1,0:T(8,128)(2,1)} %param.13) | copy-start | bytes 1572868
  201.4 19.8 %all-to-all-start.1 = ((bf16[64,4,128]{2,1,0:T(4,128)(2,1)}), bf16[64,4,128]{2,1,0:T(4,128)(2,1)S(1)}, u32[]{:S(2)}, u32[]{:S(2)}) async-start(bf16[64,4,128]{2,1,0:T(4,128)(2,1)} %select_select_fusion.1), calls=%async_computation.3 | async-start | bytes 131072 | tf_op jit(solution)/shard_map/all_to_all | solution.py:201
  230.9 6.3 %copy-start.3 = (bf16[128,8,128]{0,2,1:T(8,128)(2,1)S(1)}, bf16[128,8,128]{0,2,1:T(8,128)(2,1)}, u32[]{:S(2)}) copy-start(bf16[128,8,128]{0,2,1:T(8,128)(2,1)} %get-tuple-element.439) | copy-start | bytes 786436
  230.9 8.1 %copy-start.8 = (bf16[128,256]{1,0:T(8,128)(2,1)S(1)}, bf16[128,256]{1,0:T(8,128)(2,1)}, u32[]{:S(2)}) copy-start(bf16[128,256]{1,0:T(8,128)(2,1)} %reduce-scatter.5.cloned.1.call-done) | copy-start | bytes 196612
  230.9 57.5 %all-to-all-start.2 = ((bf16[64,8,2048]{2,1,0:T(8,128)(2,1)}), bf16[64,8,2048]{2,1,0:T(8,128)(2,1)}, u32[]{:S(2)}, u32[]{:S(2)}) async-start(bf16[64,8,2048]{2,1,0:T(8,128)(2,1)} %fusion.58), calls=%async_computation.4 | async-start | bytes 4194304 | tf_op jit(solution)/shard_map/all_to_all | solution.py:65
Sparse Core Ops, SparseCore 0:
  11.5 34.1 reduce-scatter.2
  163.4 35.2 reduce-scatter.4

commit v2 on v1

v2 whole, which is shorter than its diff:
```python
import math

import jax
import jax.numpy as jnp
import numpy as np
from jax import lax
from jax.experimental import pallas as pl
from jax.experimental.pallas import tpu as pltpu
from jax.sharding import PartitionSpec as P

F32, BF16 = jnp.float32, jnp.bfloat16
HEAD = 128
THETA = 500000.0
MESH = pl.DeviceIdType.MESH
Q, KV, DO, PART, GATHER, TERMS, ZBACK, CBACK, KEYS, TOK, ZSUM, XSUM = range(12)
PHASES = 12
L_TOK, L_W, L_Q, L_V, L_DO, L_ATT, L_QG, L_VG, L_FG, L_KWG = range(10)


def iota(shape, axis):
    return lax.broadcasted_iota(jnp.int32, shape, axis)


def one_hot(mask):
    return jnp.where(mask, 1.0, 0.0).astype(BF16)


def mm(a, b):
    return lax.dot_general(a, b, (((1,), (0,)), ((), ())), preferred_element_type=F32)


def mm_nt(a, b):
    return lax.dot_general(a, b, (((1,), (1,)), ((), ())), preferred_element_type=F32)


def mm_tn(a, b):
    return lax.dot_general(a, b, (((0,), (0,)), ((), ())), preferred_element_type=F32)


def rows(start, size, step):
    return pl.ds(pl.multiple_of(start, step), size)


def kernel(
    plan, lengths, freq, tokens_h, q_h, v_h, do_h, w_h,
    att_h, qg_h, vg_h, fg_h, kwg_h,
    tok, qv, vv, dov, wv, smat, rmat,
    send_q, recv_q, send_do, recv_do, send_kv, recv_kv, part_s, part_r,
    kv_all, q_ctx, do_ctx, att, qg, terms, terms_s, terms_r,
    zs, zr, cs, cr, kgs, kgr, toks, sum_s, sum_r, xs, xr, vg, fg, kwg,
    local_sem, send_sem, recv_sem,
):
    d, c, t = lax.axis_index("dp"), lax.axis_index("ctx"), lax.axis_index("tensor")
    me = d * 8 + c
    x, y = lax.div(c, 4), lax.rem(c, 4)

    barrier = pltpu.get_barrier_semaphore()

    def greet_group(k, carry):
        peer = lax.rem(me + k, 64)
        pl.semaphore_signal(
            barrier, inc=1, device_id=(lax.div(peer, 8), lax.rem(peer, 8), t), device_id_type=MESH
        )
        return carry

    def greet_heads(k, carry):
        pl.semaphore_signal(
            barrier,
            inc=1,
            device_id=(d, lax.rem(k, 8), lax.rem(t + 1 + lax.div(k, 8), 4)),
            device_id_type=MESH,
        )
        return carry

    lax.fori_loop(1, 64, greet_group, 0)
    lax.fori_loop(0, 24, greet_heads, 0)

    def load(src, dst, k):
        return pltpu.make_async_copy(src, dst, local_sem.at[k])

    loads = {
        L_Q: load(q_h, qv, L_Q),
        L_TOK: load(tokens_h, tok, L_TOK),
        L_W: load(w_h, wv, L_W),
        L_V: load(v_h, vv, L_V),
        L_DO: load(do_h, dov, L_DO),
    }
    for item in loads.values():
        item.start()

    def remote(src, dst, phase, target):
        return pltpu.make_async_remote_copy(
            src_ref=src,
            dst_ref=dst,
            send_sem=send_sem.at[phase],
            recv_sem=recv_sem.at[phase],
            device_id=target,
            device_id_type=MESH,
        )

    def bulk(view, phase):
        return remote(view, view, phase, (d, lax.rem(c + 1, 8), t))

    row = plan[pl.ds(me, 1), :].astype(F32)
    spread = one_hot(lax.div(lax.rem(iota((32, 512), 1), 128), 4) == iota((32, 512), 0))
    dest = mm(jnp.broadcast_to(row, (128, 32)).astype(BF16), spread)
    r_row, r_col = iota((128, 512), 0), iota((128, 512), 1)
    fits = (lax.rem(r_row, 4) == lax.rem(r_col, 4)) & (
        lax.div(lax.rem(r_row, 16), 4) == lax.div(r_col, 128)
    )
    dest = jnp.where(fits, dest, -1.0)
    slot_row = lax.div(r_row, 16)

    loads[L_Q].wait()
    pl.semaphore_wait(barrier, 87)

    def send_slots(source, target, width, phase, off):
        g = lax.rem(d + off, 8)

        def one(k, carry):
            cc = lax.rem(c + k, 8)
            j = g * 8 + cc

            @pl.when((off > 0) | (k > 0))
            def _():
                remote(
                    source.at[rows(j * 16, 16, 16), :],
                    target.at[rows(me * 16, 16, 16), :],
                    phase,
                    (g, cc, t),
                ).start()

            return carry

        lax.fori_loop(0, 8, one, 0)

    def own_slot(source, target):
        target[rows(me * 16, 16, 16), :] = source[rows(me * 16, 16, 16), :]

    def send_queries(off, carry):
        g = lax.rem(d + off, 8)
        chosen = one_hot(dest == (slot_row + g * 8).astype(F32))
        smat[rows(g * 128, 128, 128), :] = chosen
        total = mm(chosen[:, 0:128], qv[:, 0:256])
        for ch in range(1, 4):
            total += mm(chosen[:, ch * 128 : ch * 128 + 128], qv[:, ch * 256 : ch * 256 + 256])
        send_q[rows(g * 128, 128, 128), :] = total.astype(BF16)
        send_slots(send_q, recv_q, 256, Q, off)
        return carry

    lax.fori_loop(0, 8, send_queries, 0)
    own_slot(send_q, recv_q)

    loads[L_TOK].wait()
    loads[L_W].wait()
    for h in range(4):
        part_s[h] = mm_nt(tok[...], wv[h * 128 : h * 128 + 128, :])

    def send_part(k, carry):
        tt = lax.rem(t + k, 4)
        remote(part_s.at[tt], part_r.at[t], PART, (d, c, tt)).start()
        return carry

    lax.fori_loop(1, 4, send_part, 0)
    part_r[pl.ds(t, 1)] = part_s[pl.ds(t, 1)]

    lens = lengths[...]
    high = lax.div(lens, 32)
    low = lens - high * 32
    upper = one_hot(iota((16, 16), 0) <= iota((16, 16), 1))
    ends = mm(high.astype(F32).astype(BF16), upper) * 32.0 + mm(low.astype(F32).astype(BF16), upper)
    mine = iota((8, 16), 0) == d
    end_row = jnp.sum(jnp.where(mine, ends, 0.0), axis=0, keepdims=True)
    len_row = jnp.sum(jnp.where(mine, lens.astype(F32), 0.0), axis=0, keepdims=True)
    position = (c * 128 + iota((128, 16), 0)).astype(F32)
    seq_start = jnp.sum(jnp.where(end_row <= position, len_row, 0.0), axis=1, keepdims=True)
    angle = (position[:, 0:1] - seq_start) * freq[...]
    cosine = jnp.cos(angle)
    sine = jnp.sin(angle)
    signed = jnp.where(iota((128, 128), 1) < 64, -sine, sine)

    loads[L_V].wait()
    loads[L_DO].wait()

    def send_cotangents(off, carry):
        g = lax.rem(d + off, 8)
        chosen = smat[rows(g * 128, 128, 128), :]
        total = mm(chosen[:, 0:128], dov[:, 0:256])
        for ch in range(1, 4):
            total += mm(chosen[:, ch * 128 : ch * 128 + 128], dov[:, ch * 256 : ch * 256 + 256])
        send_do[rows(g * 128, 128, 128), :] = total.astype(BF16)
        return carry

    lax.fori_loop(0, 8, send_cotangents, 0)

    bulk(part_r.at[pl.ds(0, 3)], PART).wait_recv()
    key_proj = (part_r[0] + part_r[1] + part_r[2] + part_r[3]).astype(BF16)

    def send_keys(off, carry):
        g = lax.rem(d + off, 8)
        chosen = smat[rows(g * 128, 128, 128), 0:256]
        total = mm(chosen[:, 0:128], key_proj) + mm(chosen[:, 128:256], vv[...])
        send_kv[rows(g * 128, 128, 128), :] = total.astype(BF16)
        send_slots(send_kv, recv_kv, 128, KV, off)
        return carry

    lax.fori_loop(0, 8, send_keys, 0)
    own_slot(send_kv, recv_kv)

    def start_cotangents(off, carry):
        send_slots(send_do, recv_do, 256, DO, off)
        return carry

    lax.fori_loop(0, 8, start_cotangents, 0)
    own_slot(send_do, recv_do)

    def send_tokens(k, carry):
        cc = lax.rem(c + k, 8)
        half = lax.div(cc, 4) * 1024
        remote(
            tok.at[:, rows(half, 1024, 128)],
            toks.at[rows(c * 128, 128, 128), :],
            TOK,
            (d, cc, t),
        ).start()
        return carry

    lax.fori_loop(1, 8, send_tokens, 0)
    toks[rows(c * 128, 128, 128), :] = tok[:, rows(x * 1024, 1024, 128)]

    live = jnp.sum(jnp.where(plan[...] == me, 1.0, 0.0), axis=1, keepdims=True)
    live = jnp.broadcast_to(live, (64, 128)).astype(BF16)
    slot = lax.div(iota((64, 1024), 1), 16)
    before = one_hot(iota((64, 1024), 0) < slot)
    same = one_hot(iota((64, 1024), 0) == slot)
    col = iota((128, 1024), 1)
    spot = mm_tn(live, before) * 4.0 + (
        lax.rem(col, 4) + 128 * lax.div(lax.rem(col, 16), 4)
    ).astype(F32)
    spot = jnp.where(mm_tn(live, same) > 0.5, spot, -1.0)
    for ch in range(4):
        rmat[ch * 128 : ch * 128 + 128, :] = one_hot(
            spot == (iota((128, 1024), 0) + ch * 128).astype(F32)
        )
    slot4 = lax.div(iota((64, 256), 1), 4)
    spot4 = mm_tn(live, one_hot(iota((64, 256), 0) < slot4)) * 4.0 + lax.rem(
        iota((128, 256), 1), 4
    ).astype(F32)
    spot4 = jnp.where(mm_tn(live, one_hot(iota((64, 256), 0) == slot4)) > 0.5, spot4, -1.0)
    back = one_hot(spot4 == iota((128, 256), 0).astype(F32))

    bulk(recv_kv.at[pl.ds(0, 1008)], KV).wait_recv()
    pair = mm(rmat[0:256, :], recv_kv[...])
    raw = pair[0:128]
    keys = raw * cosine + pltpu.roll(raw, 64, 1) * signed
    kv_all[rows(c * 128, 128, 128), 0:128] = keys.astype(BF16)
    kv_all[rows(c * 128, 128, 128), 128:256] = pair[128:256].astype(BF16)

    def send_gather(k, carry):
        cc = lax.rem(c + k, 8)
        block = kv_all.at[rows(c * 128, 128, 128), :]
        remote(block, block, GATHER, (d, cc, t)).start()
        return carry

    lax.fori_loop(1, 8, send_gather, 0)

    bulk(recv_q.at[pl.ds(0, 1008)], Q).wait_recv()
    for ch in range(4):
        q_ctx[:, ch * 256 : ch * 256 + 256] = mm(
            rmat[ch * 128 : ch * 128 + 128, :], recv_q[...]
        ).astype(BF16)
    bulk(recv_do.at[pl.ds(0, 1008)], DO).wait_recv()
    for ch in range(4):
        do_ctx[:, ch * 256 : ch * 256 + 256] = mm(
            rmat[ch * 128 : ch * 128 + 128, :], recv_do[...]
        ).astype(BF16)
    bulk(kv_all.at[pl.ds(0, 896)], GATHER).wait_recv()

    scale = HEAD**-0.5
    key_at = iota((128, 1024), 1).astype(F32)
    visible = (key_at <= (c * 128 + iota((128, 1024), 0)).astype(F32)) & (key_at >= seq_start)
    terms[...] = jnp.zeros_like(terms)

    def attend(h, carry):
        here = rows(h * 128, 128, 128)
        query, grad = q_ctx[:, here], do_ctx[:, here]
        key, value = kv_all[:, 0:128], kv_all[:, 128:256]
        scores = jnp.where(visible, mm_nt(query, key) * scale, -1e30)
        weight = jnp.where(visible, jnp.exp(scores - jnp.max(scores, axis=1, keepdims=True)), 0.0)
        prob = weight * (1.0 / jnp.sum(weight, axis=1, keepdims=True))
        rounded = prob.astype(BF16)
        out = mm(rounded, value).astype(BF16)
        att[:, here] = out
        delta = jnp.sum(grad.astype(F32) * out.astype(F32), axis=1, keepdims=True)
        dscore = (prob * (mm_nt(grad, value) - delta)).astype(BF16)
        qg[:, here] = (mm(dscore, key) * scale).astype(BF16)
        terms[:, 0:128] += mm_tn(dscore, query)
        terms[:, 128:256] += mm_tn(rounded, grad)
        return carry

    lax.fori_loop(0, 8, attend, 0)
    stores = {L_ATT: load(att, att_h, L_ATT), L_QG: load(qg, qg_h, L_QG)}
    stores[L_ATT].start()
    stores[L_QG].start()

    terms_s[...] = terms[...].astype(BF16)

    def send_terms(k, carry):
        cc = lax.rem(c + k, 8)
        remote(
            terms_s.at[rows(cc * 128, 128, 128), :],
            terms_r.at[rows(c * 128, 128, 128), :],
            TERMS,
            (d, cc, t),
        ).start()
        return carry

    lax.fori_loop(1, 8, send_terms, 0)
    terms_r[rows(c * 128, 128, 128), :] = terms_s[rows(c * 128, 128, 128), :]
    out_row, in_row = iota((256, 256), 0), iota((256, 256), 1)
    regroup = one_hot(
        (lax.div(out_row, 32) == lax.div(lax.rem(in_row, 32), 4))
        & (lax.div(lax.rem(out_row, 32), 4) == lax.div(in_row, 32))
        & (lax.rem(out_row, 4) == lax.rem(in_row, 4))
    )
    line = iota((256, 128), 0)
    source = lax.div(lax.rem(line, 32), 4) * 8 + lax.div(line, 32)
    spread4 = one_hot(lax.div(iota((32, 128), 1), 4) == iota((32, 128), 0))
    dest4 = mm(jnp.broadcast_to(row, (256, 32)).astype(BF16), spread4)
    collect = one_hot(
        (dest4 == source.astype(F32)) & (lax.rem(line, 4) == lax.rem(iota((256, 128), 1), 4))
    )
    new_col, old = iota((512, 512), 1), iota((512, 512), 0)
    reorder = one_hot(
        old
        == lax.rem(lax.div(new_col, 16), 8) * 64
        + lax.rem(lax.div(new_col, 8), 2) * 32
        + lax.div(new_col, 128) * 8
        + lax.rem(new_col, 8)
    )
    bulk(terms_r.at[pl.ds(0, 896)], TERMS).wait_recv()
    owned = terms_r[0:128, :].astype(F32)
    for k in range(1, 8):
        owned += terms_r[k * 128 : k * 128 + 128, :].astype(F32)
    rot_grad = owned[:, 0:128] * scale
    vg[...] = owned[:, 128:256].astype(BF16)
    stores[L_VG] = load(vg, vg_h, L_VG)
    stores[L_VG].start()
    key_grad = (rot_grad * cosine - pltpu.roll(rot_grad, 64, 1) * signed).astype(BF16)

    zs[...] = mm_tn(back, key_grad).astype(BF16)

    def send_z(k, carry):
        g = lax.rem(d + k, 8)
        remote(
            zs.at[rows(g * 32, 32, 32), :], zr.at[rows(d * 32, 32, 32), :], ZBACK, (g, c, t)
        ).start()
        return carry

    lax.fori_loop(1, 8, send_z, 0)
    zr[rows(d * 32, 32, 32), :] = zs[rows(d * 32, 32, 32), :]
    bulk(zr.at[pl.ds(0, 224)], ZBACK).wait_recv()
    cs[...] = mm(regroup, zr[...]).astype(BF16)
    spot_here = t * 256 + c * 32

    def send_c(k, carry):
        cc = lax.rem(c + lax.rem(k, 8), 8)
        tt = lax.rem(t + lax.div(k, 8), 4)
        remote(
            cs.at[rows(cc * 32, 32, 32), :], cr.at[rows(spot_here, 32, 32), :], CBACK, (d, cc, tt)
        ).start()
        return carry

    lax.fori_loop(1, 32, send_c, 0)
    cr[rows(spot_here, 32, 32), :] = cs[rows(c * 32, 32, 32), :]
    bulk(cr.at[pl.ds(0, 992)], CBACK).wait_recv()
    all_grads = jnp.concatenate(
        [mm_tn(collect, cr[h * 256 : h * 256 + 256, :]).astype(BF16) for h in range(4)], axis=1
    )

    moved = mm(all_grads, reorder).astype(BF16)
    for k in range(4):
        kgs[k] = moved[:, k * 128 : k * 128 + 128]

    def send_grads(k, carry):
        cc = lax.rem(c + k, 8)
        remote(
            kgs.at[lax.rem(cc, 4)], kgr.at[rows(c * 128, 128, 128), :], KEYS, (d, cc, t)
        ).start()
        return carry

    lax.fori_loop(1, 8, send_grads, 0)
    kgr[rows(c * 128, 128, 128), :] = kgs[y]
    for k in range(4):
        fg[:, k * 512 : k * 512 + 512] = mm(
            all_grads, wv[:, k * 512 : k * 512 + 512]
        ).astype(BF16)
    stores[L_FG] = load(fg, fg_h, L_FG)
    stores[L_FG].start()
    bulk(toks.at[pl.ds(0, 896)], TOK).wait_recv()
    bulk(kgr.at[pl.ds(0, 896)], KEYS).wait_recv()
    sum_s[...] = mm_tn(kgr[...], toks[...]).astype(BF16)

    def send_sums(k, carry):
        g = lax.rem(d + k, 8)
        remote(
            sum_s.at[rows(g * 16, 16, 16), :], sum_r.at[rows(d * 16, 16, 16), :], ZSUM, (g, c, t)
        ).start()
        return carry

    lax.fori_loop(1, 8, send_sums, 0)
    sum_r[rows(d * 16, 16, 16), :] = sum_s[rows(d * 16, 16, 16), :]
    bulk(sum_r.at[pl.ds(0, 112)], ZSUM).wait_recv()
    added = sum_r[0:16, :].astype(F32)
    for k in range(1, 8):
        added += sum_r[k * 16 : k * 16 + 16, :].astype(F32)
    xs[0] = added[0:8]
    xs[1] = added[8:16]
    swap = remote(xs.at[1 - x], xr, XSUM, (d, lax.rem(c + 4, 8), t))
    swap.start()
    kwg[:, rows(x * 1024, 1024, 128)] = xs[x]
    swap.wait_recv()
    kwg[:, rows((1 - x) * 1024, 1024, 128)] = xr[...]
    stores[L_KWG] = load(kwg, kwg_h, L_KWG)
    stores[L_KWG].start()

    bulk(send_q.at[pl.ds(0, 1008)], Q).wait_send()
    bulk(send_kv.at[pl.ds(0, 1008)], KV).wait_send()
    bulk(send_do.at[pl.ds(0, 1008)], DO).wait_send()
    bulk(part_s.at[pl.ds(0, 3)], PART).wait_send()
    bulk(kv_all.at[pl.ds(0, 896)], GATHER).wait_send()
    bulk(terms_s.at[pl.ds(0, 896)], TERMS).wait_send()
    bulk(zs.at[pl.ds(0, 224)], ZBACK).wait_send()
    bulk(cr.at[pl.ds(0, 992)], CBACK).wait_send()
    bulk(kgr.at[pl.ds(0, 896)], KEYS).wait_send()
    bulk(toks.at[pl.ds(0, 896)], TOK).wait_send()
    bulk(sum_s.at[pl.ds(0, 112)], ZSUM).wait_send()
    swap.wait_send()
    for item in stores.values():
        item.wait()


def shards(tokens, queries, values, out_grad, key_weight, plan, lengths):
    half = np.arange(128) % 64
    freq = np.exp(-(half.astype(np.float32) * np.float32(2.0 / HEAD)) * np.float32(math.log(THETA)))
    freq = jnp.asarray(freq.astype(np.float32).reshape(1, 128))
    vmem = pl.BlockSpec(memory_space=pltpu.VMEM)
    hbm = pl.BlockSpec(memory_space=pl.ANY)
    scratch = [
        ((128, 2048), BF16), ((128, 1024), BF16), ((128, 128), BF16), ((128, 1024), BF16),
        ((512, 2048), BF16), ((1024, 512), BF16), ((512, 1024), BF16),
        ((1024, 256), BF16), ((1024, 256), BF16), ((1024, 256), BF16), ((1024, 256), BF16),
        ((1024, 128), BF16), ((1024, 128), BF16), ((4, 128, 128), F32), ((4, 128, 128), F32),
        ((1024, 256), BF16), ((128, 1024), BF16), ((128, 1024), BF16), ((128, 1024), BF16),
        ((128, 1024), BF16), ((1024, 256), F32), ((1024, 256), BF16), ((1024, 256), BF16),
        ((256, 128), BF16), ((256, 128), BF16), ((256, 128), BF16), ((1024, 128), BF16),
        ((4, 128, 128), BF16), ((1024, 128), BF16), ((1024, 1024), BF16), ((128, 1024), BF16),
        ((128, 1024), BF16), ((2, 8, 1024), F32), ((8, 1024), F32), ((128, 128), BF16),
        ((128, 2048), BF16), ((8, 2048), F32),
    ]
    return pl.pallas_call(
        kernel,
        out_shape=(
            jax.ShapeDtypeStruct((128, 1024), BF16),
            jax.ShapeDtypeStruct((128, 1024), BF16),
            jax.ShapeDtypeStruct((128, 128), BF16),
            jax.ShapeDtypeStruct((128, 2048), BF16),
            jax.ShapeDtypeStruct((8, 2048), F32),
        ),
        in_specs=[vmem] * 3 + [hbm] * 5,
        out_specs=(hbm,) * 5,
        scratch_shapes=[pltpu.VMEM(shape, dtype) for shape, dtype in scratch]
        + [
            pltpu.SemaphoreType.DMA((10,)),
            pltpu.SemaphoreType.DMA((PHASES,)),
            pltpu.SemaphoreType.DMA((PHASES,)),
        ],
        compiler_params=pltpu.CompilerParams(
            collective_id=0, has_side_effects=True, vmem_limit_bytes=48 * 1024 * 1024
        ),
    )(plan, lengths, freq, tokens, queries, values, out_grad, key_weight)


def solution(mesh):
    both = P(("dp", "ctx"), "tensor")
    return jax.shard_map(
        shards,
        mesh=mesh,
        in_specs=(both, both, both, both, P(None, "tensor"), P(), P()),
        out_specs=(both,) * 5,
        check_vma=False,
    )
```

time: 299 us -> 129 us (0.43)
  waiting for transfers between devices: 155 us -> 0 us
  Pallas kernels: 0 us -> 117 us
  blocking collectives: 36 us -> 0 us
  starting transfers between devices: 28 us -> 0 us
  matrix products: 18.5 us -> 0 us
  other arithmetic: 15.7 us -> 0 us
  local copies, waits for them, and re-layouts: 25.5 us -> 10.9 us
  between operations: 14.4 us -> 0.65 us
  loops' own time: 4.5 us -> 0 us
    pallas_call x0 -> x1, Pallas kernels: none -> 117 us  [shards(): pl.pallas_call(kernel, out_shape=(jax.ShapeDtypeStruct((128, 1024), BF16)...]
    all_to_all x3 -> x0, waiting for transfers between devices: 86.3 us -> none  [the longest x1 47.6 us: weight_grads(): lax.all_to_all(terms.astype(jnp.bfloat16), ('dp', 'ctx'), split_axis=0, c...]
    reduce_scatter x2 -> x0, waiting for transfers between devices: 68.8 us -> none  [the longest x1 35.4 us: shards(): lax.psum_scatter(group_terms.astype(jnp.bfloat16), 'ctx', scatter_dimensi...]
    all_gather x2 -> x0, blocking collectives: 36 us -> none  [the longest x1 29.1 us: shards(): lax.all_gather(jnp.concatenate([keys, value_ctx], axis=1), 'ctx', axis=0,...]
    all_to_all x3 -> x0, starting transfers between devices: 27.9 us -> none  [the longest x1 11.7 us: shards(): lax.all_to_all(send_out(grouped), ('dp', 'ctx'), split_axis=0, concat_axi...]
    dot_general x17 -> x0, matrix products: 18.5 us -> none  [the longest x2 5.21 us: output_step(): jnp.einsum('hqk,kd->qhd', weights, value_tile, preferred_element_type=jnp...]
    unnamed x20, local copies, waits for them, and re-layouts: 3.74 us -> 10.9 us
    gather x5 -> x0, local copies, waits for them, and re-layouts: 7.07 us -> none  [the longest x3 3.88 us: arrange(): jnp.take(received, chosen_slab, axis=0).reshape(-1, received.shape[-1])]
  transfers between devices with their start and end apart: 5 -> 0, of which waited for: 5 -> 0; matrix products, arithmetic and copies ran while one was open for 2% -> 0% of each run, Pallas kernels for 0% -> 0%
where the time goes in v2:
time: 129 us; the launch traced here: 128 us
  Pallas kernels  117 us (91%)
  local copies, waits for them, and re-layouts  10.9 us (8%)
    pallas_call x1, Pallas kernels, shards(): pl.pallas_call(kernel, out_shape=(jax.ShapeDtypeStruct((128, 1024), BF16)...  117 us
    unnamed x20, local copies, waits for them, and re-layouts  10.9 us

profile of v2, /device:TPU:2, one launch (start us, length us, event | category | flops | bytes accessed | tf_op | source)
XLA Modules:
  0.0 128.5 jit_solution(8595156542933035368)
XLA Ops:
  0.6 0.8 copy.13.plan
  1.4 0.0 copy-start
  1.4 1.6 %copy-done = bf16[512,2048]{1,0:T(8,128)(2,1)S(1)} copy-done((bf16[512,2048]{1,0:T(8,128)(2,1)S(1)}, bf16[512,2048]{1,0:T(8,128)(2,1)}, u32[]{:S(2)}) %copy-start) | copy-done | bytes 2097176
  3.0 0.0 copy-start.1
  3.0 1.0 copy-done.1
  4.1 0.0 copy-start.2
  4.1 0.9 copy-done.2
  5.0 0.0 copy-start.3
  5.0 0.9 copy-done.3
  6.0 0.0 copy-start.4
  6.0 0.8 copy-done.4
  6.7 0.0 copy-start.5
  6.7 0.7 copy-done.5
  7.4 0.0 copy-start.6
  7.4 0.7 copy-done.6
  8.1 117.0 %shard_map.119 = (bf16[128,1024]{1,0:T(8,128)(2,1)S(1)}, bf16[128,1024]{1,0:T(8,128)(2,1)S(1)}, bf16[128,128]{1,0:T(8,128)(2,1)S(1)}, bf16[128,2048]{1,0:T(8,128)(2,1)S(1)}, f32[8,2048]{1,0:T(8,128)S(1)}) custom-call(s32[64,32]{1,0:T(8,128)S(1)} %copy.13.plan, s32[8,16]{1,0:T(8,128)S(1)} %copy-done.5, f32[1,128]{1,0:T(1,128)S(1)} %copy-done.6, ...), custom_call_target="tpu_custom_call" | custom-call | tf_op jit(solution)/shard_map/pallas_call | solution.py:461
  125.0 0.7 copy.19
  125.8 0.7 copy.20
  126.5 0.6 copy.21
  127.1 0.8 copy.22
  127.9 0.6 copy.23
Async XLA Ops:
  1.4 1.6 %copy-start = (bf16[512,2048]{1,0:T(8,128)(2,1)S(1)}, bf16[512,2048]{1,0:T(8,128)(2,1)}, u32[]{:S(2)}) copy-start(bf16[512,2048]{1,0:T(8,128)(2,1)} %w_h.1) | copy-start | bytes 6291460
  3.0 1.0 copy-start.1
  4.1 0.9 copy-start.2
  5.0 0.9 copy-start.3
  6.0 0.8 copy-start.4
  6.7 0.7 copy-start.5
  7.4 0.7 copy-start.6

commit v3 on v2

v3 whole, which is shorter than its diff:
```python
import math

import jax
import jax.numpy as jnp
import numpy as np
from jax import lax
from jax.experimental import pallas as pl
from jax.experimental.pallas import tpu as pltpu
from jax.sharding import PartitionSpec as P

F32, BF16 = jnp.float32, jnp.bfloat16
HEAD = 128
THETA = 500000.0
MESH = pl.DeviceIdType.MESH
Q, ZKV, CKV, DO, PART, GATHER, TERMS, ZBACK, CBACK, KEYS, TOK, ZSUM, YSUM = range(13)
PHASES = 13
L_TOK, L_W, L_Q, L_V, L_DO, L_ATT, L_QG, L_VG, L_FG, L_KWG = range(10)


def iota(shape, axis):
    return lax.broadcasted_iota(jnp.int32, shape, axis)


def one_hot(mask):
    return jnp.where(mask, 1.0, 0.0).astype(BF16)


def mm(a, b):
    return lax.dot_general(a, b, (((1,), (0,)), ((), ())), preferred_element_type=F32)


def mm_nt(a, b):
    return lax.dot_general(a, b, (((1,), (1,)), ((), ())), preferred_element_type=F32)


def mm_tn(a, b):
    return lax.dot_general(a, b, (((0,), (0,)), ((), ())), preferred_element_type=F32)


def rows(start, size, step):
    return pl.ds(pl.multiple_of(start, step), size)


def kernel(
    plan, lengths, freq, tokens_h, q_h, v_h, do_h, w_h,
    att_h, qg_h, vg_h, fg_h, kwg_h,
    tok, qv, vv, dov, wv, smat, rmat,
    send_q, recv_q, send_do, recv_do, zkv_s, zkv_r, ckv_s, ckv_r, part_s, part_r,
    kv_all, qs, dos, prob, weights, dscores, att, att_t, delta, qg, terms_s, terms_r,
    zs, zr, cs, cr, kgs, kgr, toks, sum_s, sum_r, ys, yr, vg, fg, kwg,
    local_sem, send_sem, recv_sem, term_sem,
):
    d, c, t = lax.axis_index("dp"), lax.axis_index("ctx"), lax.axis_index("tensor")
    me = d * 8 + c
    x, y = lax.div(c, 4), lax.rem(c, 4)

    barrier = pltpu.get_barrier_semaphore()

    def greet_group(k, carry):
        peer = lax.rem(me + k, 64)
        pl.semaphore_signal(
            barrier, inc=1, device_id=(lax.div(peer, 8), lax.rem(peer, 8), t), device_id_type=MESH
        )
        return carry

    def greet_heads(k, carry):
        pl.semaphore_signal(
            barrier,
            inc=1,
            device_id=(d, lax.rem(k, 8), lax.rem(t + 1 + lax.div(k, 8), 4)),
            device_id_type=MESH,
        )
        return carry

    lax.fori_loop(1, 64, greet_group, 0)
    lax.fori_loop(0, 24, greet_heads, 0)

    def local(src, dst, k):
        return pltpu.make_async_copy(src, dst, local_sem.at[k])

    loads = {
        L_Q: local(q_h, qv, L_Q),
        L_TOK: local(tokens_h, tok, L_TOK),
        L_W: local(w_h, wv, L_W),
        L_V: local(v_h, vv, L_V),
        L_DO: local(do_h, dov, L_DO),
    }
    for item in loads.values():
        item.start()
    stores = {}

    def remote(src, dst, phase, target):
        return pltpu.make_async_remote_copy(
            src_ref=src,
            dst_ref=dst,
            send_sem=send_sem.at[phase],
            recv_sem=recv_sem.at[phase],
            device_id=target,
            device_id_type=MESH,
        )

    sizes = {
        Q: recv_q.at[pl.ds(0, 1008)],
        ZKV: zkv_r.at[pl.ds(0, 224)],
        CKV: ckv_r.at[pl.ds(0, 224)],
        DO: recv_do.at[pl.ds(0, 1008)],
        PART: part_r.at[pl.ds(0, 3)],
        GATHER: kv_all.at[pl.ds(0, 896)],
        ZBACK: zr.at[pl.ds(0, 224)],
        CBACK: kgr.at[pl.ds(0, 496)],
        KEYS: kgr.at[pl.ds(0, 896)],
        TOK: toks.at[pl.ds(0, 896)],
        ZSUM: sum_r.at[pl.ds(0, 224)],
        YSUM: yr.at[pl.ds(0, 3)],
    }
    unsent, unread = set(), set()

    def started(phase):
        unsent.add(phase)
        unread.add(phase)

    def bulk(phase):
        return remote(sizes[phase], sizes[phase], phase, (d, lax.rem(c + 1, 8), t))

    def arrived(phase):
        unread.discard(phase)
        bulk(phase).wait_recv()

    def term_copy(owner, k):
        return pltpu.make_async_remote_copy(
            src_ref=terms_s.at[rows(owner * 128, 128, 128), :],
            dst_ref=terms_r.at[rows(c * 128, 128, 128), :],
            send_sem=term_sem.at[0, owner],
            recv_sem=term_sem.at[1, c if k is None else k],
            device_id=(d, owner, t),
            device_id_type=MESH,
        )

    def finish():
        for phase in sorted(unread):
            bulk(phase).wait_recv()
        for phase in sorted(unsent):
            bulk(phase).wait_send()
        for item in (*loads.values(), *stores.values()):
            item.wait()

    row = jnp.sum(jnp.where(iota((32, 64), 1) == me, plan[...].astype(F32), 0.0), axis=1, keepdims=True)
    row = jnp.broadcast_to(row, (32, 256)).astype(BF16)
    spread = one_hot(lax.div(lax.rem(iota((32, 512), 1), 128), 4) == iota((32, 512), 0))
    dest = mm_tn(row, spread)
    r_row, r_col = iota((128, 512), 0), iota((128, 512), 1)
    fits = (lax.rem(r_row, 4) == lax.rem(r_col, 4)) & (
        lax.div(lax.rem(r_row, 16), 4) == lax.div(r_col, 128)
    )
    slotted = jnp.where(fits, dest[0:128], -1.0) - lax.div(r_row, 16).astype(F32)
    for g in range(8):
        smat[g * 128 : g * 128 + 128, :] = one_hot(slotted == g * 8.0)

    def stage(source):
        total = mm(smat[:, 0:128], source[:, 0:256])
        for ch in range(1, 4):
            total += mm(smat[:, ch * 128 : ch * 128 + 128], source[:, ch * 256 : ch * 256 + 256])
        return total.astype(BF16)

    loads.pop(L_Q).wait()
    send_q[...] = stage(qv)
    pl.semaphore_wait(barrier, 87)

    def send_slots(source, target, phase):
        def one(k, carry):
            peer = lax.rem(me + k, 64)
            remote(
                source.at[rows(peer * 16, 16, 16), :],
                target.at[rows(me * 16, 16, 16), :],
                phase,
                (lax.div(peer, 8), lax.rem(peer, 8), t),
            ).start()
            return carry

        lax.fori_loop(1, 64, one, 0)
        started(phase)
        target[rows(me * 16, 16, 16), :] = source[rows(me * 16, 16, 16), :]

    send_slots(send_q, recv_q, Q)

    loads.pop(L_TOK).wait()
    loads.pop(L_W).wait()
    for h in range(4):
        part_s[h] = mm_nt(tok[...], wv[h * 128 : h * 128 + 128, :])

    def send_part(k, carry):
        tt = lax.rem(t + k, 4)
        remote(part_s.at[tt], part_r.at[t], PART, (d, c, tt)).start()
        return carry

    lax.fori_loop(1, 4, send_part, 0)
    started(PART)
    part_r[pl.ds(t, 1)] = part_s[pl.ds(t, 1)]

    line, column = iota((256, 128), 0), iota((256, 128), 1)
    four = lax.rem(line, 4) == lax.rem(column, 4)
    to_slots = one_hot(four & (dest[:, 0:128] == lax.div(line, 4).astype(F32)))
    out_row, in_row = iota((256, 256), 0), iota((256, 256), 1)
    regroup = one_hot(
        (lax.div(out_row, 32) == lax.div(lax.rem(in_row, 32), 4))
        & (lax.div(lax.rem(out_row, 32), 4) == lax.div(in_row, 32))
        & (lax.rem(out_row, 4) == lax.rem(in_row, 4))
    )
    hits = one_hot(plan[...] == me)
    live_row = mm(jnp.ones((128, 32), BF16), hits).astype(BF16)
    live_col = mm_tn(hits, jnp.ones((32, 128), BF16)).astype(BF16)
    lane = iota((64, 256), 1)
    sender = lax.div(lax.rem(lane, 32), 4) * 8 + lax.div(lane, 32)
    order = iota((64, 256), 0)
    spot = mm(live_row, one_hot(order < sender)) * 4.0
    spot += lax.rem(iota((128, 256), 1), 4).astype(F32)
    spot = jnp.where(mm(live_row, one_hot(order == sender)) > 0.5, spot, -1.0)
    to_rows = one_hot(spot == iota((128, 256), 0).astype(F32))

    loads.pop(L_V).wait()
    loads.pop(L_DO).wait()
    send_do[...] = stage(dov)

    lens = lengths[...]
    high = lax.div(lens, 32)
    low = lens - high * 32
    upper = one_hot(iota((16, 16), 0) <= iota((16, 16), 1))
    ends = mm(high.astype(F32).astype(BF16), upper) * 32.0 + mm(low.astype(F32).astype(BF16), upper)
    mine = iota((8, 16), 0) == d
    end_row = jnp.sum(jnp.where(mine, ends, 0.0), axis=0, keepdims=True)
    len_row = jnp.sum(jnp.where(mine, lens.astype(F32), 0.0), axis=0, keepdims=True)
    position = (c * 128 + iota((128, 16), 0)).astype(F32)
    seq_start = jnp.sum(jnp.where(end_row <= position, len_row, 0.0), axis=1, keepdims=True)
    angle = (position[:, 0:1] - seq_start) * freq[...]
    cosine = jnp.cos(angle)
    sine = jnp.sin(angle)
    signed = jnp.where(iota((128, 128), 1) < 64, -sine, sine)

    arrived(PART)
    key_proj = (part_r[0] + part_r[1] + part_r[2] + part_r[3]).astype(BF16)
    zkv_s[...] = mm(to_slots, jnp.concatenate([key_proj, vv[...]], axis=1)).astype(BF16)

    def send_blocks(source, target, phase, size):
        def one(k, carry):
            g = lax.rem(d + k, 8)
            remote(
                source.at[rows(g * size, size, size), :],
                target.at[rows(d * size, size, size), :],
                phase,
                (g, c, t),
            ).start()
            return carry

        lax.fori_loop(1, 8, one, 0)
        started(phase)
        target[rows(d * size, size, size), :] = source[rows(d * size, size, size), :]

    send_blocks(zkv_s, zkv_r, ZKV, 32)
    send_slots(send_do, recv_do, DO)

    slot = lax.div(iota((64, 1024), 1), 16)
    col = iota((128, 1024), 1)
    spot = mm(live_row, one_hot(iota((64, 1024), 0) < slot)) * 4.0 + (
        lax.rem(col, 4) + 128 * lax.div(lax.rem(col, 16), 4)
    ).astype(F32)
    spot = jnp.where(mm(live_row, one_hot(iota((64, 1024), 0) == slot)) > 0.5, spot, -1.0)
    for ch in range(4):
        rmat[ch * 128 : ch * 128 + 128, :] = one_hot(
            spot == (iota((128, 1024), 0) + ch * 128).astype(F32)
        )

    arrived(ZKV)
    ckv_s[...] = mm(regroup, zkv_r[...]).astype(BF16)

    def send_ckv(k, carry):
        cc = lax.rem(c + k, 8)
        remote(
            ckv_s.at[rows(cc * 32, 32, 32), :], ckv_r.at[rows(c * 32, 32, 32), :], CKV, (d, cc, t)
        ).start()
        return carry

    lax.fori_loop(1, 8, send_ckv, 0)
    started(CKV)
    ckv_r[rows(c * 32, 32, 32), :] = ckv_s[rows(c * 32, 32, 32), :]
    for k in range(8):

        @pl.when(k < c)
        def _():
            terms_r[k * 128 : k * 128 + 128, :] = jnp.zeros((128, 256), BF16)

    arrived(CKV)
    pair = mm(to_rows, ckv_r[...])
    raw = pair[:, 0:128]
    keys = raw * cosine + pltpu.roll(raw, 64, 1) * signed
    kv_all[rows(c * 128, 128, 128), 0:128] = keys.astype(BF16)
    kv_all[rows(c * 128, 128, 128), 128:256] = pair[:, 128:256].astype(BF16)

    def send_gather(k, carry):
        cc = lax.rem(c + k, 8)
        block = kv_all.at[rows(c * 128, 128, 128), :]
        remote(block, block, GATHER, (d, cc, t)).start()
        return carry

    lax.fori_loop(1, 8, send_gather, 0)
    started(GATHER)

    def send_tokens(k, carry):
        cc = lax.rem(c + k, 8)
        remote(
            tok.at[:, rows(lax.rem(cc, 4) * 512, 512, 128)],
            toks.at[rows(c * 128, 128, 128), :],
            TOK,
            (d, cc, t),
        ).start()
        return carry

    lax.fori_loop(1, 8, send_tokens, 0)
    started(TOK)
    toks[rows(c * 128, 128, 128), :] = tok[:, rows(y * 512, 512, 128)]

    arrived(Q)
    heads = mm(rmat[...], recv_q[...]).astype(BF16)
    for ch in range(4):
        for k in range(2):
            qs[(2 * ch + k) * 128 : (2 * ch + k) * 128 + 128, :] = heads[
                ch * 128 : ch * 128 + 128, k * 128 : k * 128 + 128
            ]
    scale = HEAD**-0.5
    key_at = iota((1024, 128), 0).astype(F32)
    query_at = (c * 128 + iota((16, 128), 1)).astype(F32)
    end_all = jnp.where(mine, ends, 0.0)
    len_all = jnp.where(mine, lens.astype(F32), 0.0)
    pick = jnp.ones((8, 128), F32)
    end_col = lax.dot_general(
        end_all, pick, (((0,), (0,)), ((), ())),
        precision=lax.Precision.HIGHEST, preferred_element_type=F32,
    )
    len_col = lax.dot_general(
        len_all, pick, (((0,), (0,)), ((), ())),
        precision=lax.Precision.HIGHEST, preferred_element_type=F32,
    )
    starts = jnp.sum(jnp.where(end_col <= query_at, len_col, 0.0), axis=0, keepdims=True)
    hidden = jnp.where((key_at <= query_at[0:1]) & (key_at >= starts), 0.0, -1e30)

    arrived(GATHER)

    def forward(h, carry):
        here = rows(h * 128, 128, 128)
        scores = mm_nt(kv_all[:, 0:128], qs[here, :]) * scale + hidden
        grown = jnp.exp(scores - jnp.max(scores, axis=0, keepdims=True))
        chance = grown * (1.0 / jnp.sum(grown, axis=0, keepdims=True))
        prob[:, here] = chance
        rounded = chance.astype(BF16)
        weights[:, here] = rounded
        out = mm_tn(kv_all[:, 128:256], rounded).astype(BF16)
        att_t[:, here] = out
        att[:, here] = out.T
        return carry

    lax.fori_loop(0, 8, forward, 0)
    stores[L_ATT] = local(att, att_h, L_ATT)
    stores[L_ATT].start()

    arrived(DO)
    heads = mm(rmat[...], recv_do[...]).astype(BF16)
    for ch in range(4):
        for k in range(2):
            h = 2 * ch + k
            block = heads[ch * 128 : ch * 128 + 128, k * 128 : k * 128 + 128]
            dos[h * 128 : h * 128 + 128, :] = block
            products = block.T.astype(F32) * att_t[:, h * 128 : h * 128 + 128].astype(F32)
            delta[:, h * 128 : h * 128 + 128] = jnp.sum(products, axis=0, keepdims=True)

    def backward(k, carry):
        chunk = lax.rem(lax.div(c, 2) + 1 + k, 4)
        here = rows(chunk * 256, 256, 256)
        grads = mm_nt(kv_all[here, 128:256], dos[...]) - delta[...]
        rounded = (prob[here, :] * grads).astype(BF16)
        dscores[here, :] = rounded
        terms_s[here, 0:128] = mm(rounded, qs[...]).astype(BF16)
        terms_s[here, 128:256] = mm(weights[here, :], dos[...]).astype(BF16)
        for part in range(2):
            owner = chunk * 2 + part

            @pl.when(owner < c)
            def _():
                term_copy(owner, None).start()

        return carry

    lax.fori_loop(0, 4, backward, 0)
    terms_r[rows(c * 128, 128, 128), :] = terms_s[rows(c * 128, 128, 128), :]

    def query_grads(h, carry):
        here = rows(h * 128, 128, 128)
        grad = mm_tn(kv_all[:, 0:128], dscores[:, here]) * scale
        qg[:, here] = grad.astype(BF16).T
        return carry

    lax.fori_loop(0, 8, query_grads, 0)
    stores[L_QG] = local(qg, qg_h, L_QG)
    stores[L_QG].start()

    before = mm(one_hot(iota((64, 64), 1) < iota((64, 64), 0)), live_col).astype(BF16)
    widen = one_hot(iota((256, 64), 1) == lax.div(iota((256, 64), 0), 4))
    spot = mm(widen, before) * 4.0 + lax.rem(line, 4).astype(F32)
    spot = jnp.where(mm(widen, live_col) > 0.5, spot, -1.0)
    back = one_hot(spot == column.astype(F32))
    spread4 = one_hot(iota((128, 32), 1) == lax.div(iota((128, 32), 0), 4))
    lane = iota((128, 256), 1)
    sender = lax.div(lax.rem(lane, 32), 4) * 8 + lax.div(lane, 32)
    collect = one_hot(
        (mm(spread4, row) == sender.astype(F32))
        & (lax.rem(lane, 4) == lax.rem(iota((128, 256), 0), 4))
    )
    new_col, old = iota((512, 512), 1), iota((512, 512), 0)
    reorder = one_hot(
        old
        == lax.div(lax.rem(new_col, 256), 32) * 64
        + lax.div(new_col, 256) * 32
        + lax.rem(new_col, 32)
    )
    for k in range(8):

        @pl.when(k > c)
        def _():
            term_copy(k, k).wait_recv()

    owned = terms_r[0:128, :].astype(F32)
    for k in range(1, 8):
        owned += terms_r[k * 128 : k * 128 + 128, :].astype(F32)
    rot_grad = owned[:, 0:128] * scale
    key_grad = (rot_grad * cosine - pltpu.roll(rot_grad, 64, 1) * signed).astype(BF16)
    zs[...] = mm(back, key_grad).astype(BF16)
    send_blocks(zs, zr, ZBACK, 32)
    vg[...] = owned[:, 128:256].astype(BF16)
    stores[L_VG] = local(vg, vg_h, L_VG)
    stores[L_VG].start()
    arrived(ZBACK)
    cs[...] = mm(regroup, zr[...]).astype(BF16)

    def send_c(k, carry):
        cc = lax.rem(c + k, 8)
        tt = lax.rem(t + lax.div(k, 8), 4)
        remote(
            cs.at[rows(cc * 32, 32, 32), :],
            cr.at[rows(c * 32, 32, 32), rows(t * 128, 128, 128)],
            CBACK,
            (d, cc, tt),
        ).start()
        return carry

    lax.fori_loop(1, 32, send_c, 0)
    started(CBACK)
    cr[rows(c * 32, 32, 32), rows(t * 128, 128, 128)] = cs[rows(c * 32, 32, 32), :]
    arrived(CBACK)
    all_grads = mm(collect, cr[...]).astype(BF16)

    moved = mm(all_grads, reorder).astype(BF16)
    for k in range(2):
        kgs[k] = moved[:, k * 256 : k * 256 + 256]

    def send_grads(k, carry):
        cc = lax.rem(c + k, 8)
        remote(
            kgs.at[lax.div(cc, 4)], kgr.at[rows(c * 128, 128, 128), :], KEYS, (d, cc, t)
        ).start()
        return carry

    lax.fori_loop(1, 8, send_grads, 0)
    started(KEYS)
    kgr[rows(c * 128, 128, 128), :] = kgs[x]
    for k in range(4):
        fg[:, k * 512 : k * 512 + 512] = mm(
            all_grads, wv[:, k * 512 : k * 512 + 512]
        ).astype(BF16)
    stores[L_FG] = local(fg, fg_h, L_FG)
    stores[L_FG].start()
    arrived(TOK)
    arrived(KEYS)
    sum_s[...] = mm_tn(kgr[...], toks[...]).astype(BF16)
    send_blocks(sum_s, sum_r, ZSUM, 32)
    arrived(ZSUM)
    added = sum_r[0:32, :].astype(F32)
    for k in range(1, 8):
        added += sum_r[k * 32 : k * 32 + 32, :].astype(F32)
    for k in range(4):
        ys[k] = added[k * 8 : k * 8 + 8]

    def send_y(k, carry):
        yy = lax.rem(y + k, 4)
        remote(ys.at[yy], yr.at[y], YSUM, (d, x * 4 + yy, t)).start()
        return carry

    lax.fori_loop(1, 4, send_y, 0)
    started(YSUM)
    yr[y] = ys[y]
    arrived(YSUM)
    for k in range(4):
        kwg[:, k * 512 : k * 512 + 512] = yr[k]
    stores[L_KWG] = local(kwg, kwg_h, L_KWG)
    stores[L_KWG].start()
    for k in range(8):

        @pl.when(k < c)
        def _():
            term_copy(k, None).wait_send()

    finish()


def copy_out(*refs):
    sem = refs[15]
    reads = [pltpu.make_async_copy(refs[k], refs[10 + k], sem.at[0, k]) for k in range(5)]
    writes = [pltpu.make_async_copy(refs[10 + k], refs[5 + k], sem.at[1, k]) for k in range(5)]
    for item in reads:
        item.start()
    for read, write in zip(reads, writes):
        read.wait()
        write.start()
    for item in writes:
        item.wait()


def shards(tokens, queries, values, out_grad, key_weight, plan, lengths):
    half = np.arange(128) % 64
    freq = np.exp(-(half.astype(np.float32) * np.float32(2.0 / HEAD)) * np.float32(math.log(THETA)))
    freq = jnp.asarray(freq.astype(np.float32).reshape(1, 128))
    vmem = pl.BlockSpec(memory_space=pltpu.VMEM)
    hbm = pl.BlockSpec(memory_space=pl.ANY)
    scratch = [
        ((128, 2048), BF16), ((128, 1024), BF16), ((128, 128), BF16), ((128, 1024), BF16),
        ((512, 2048), BF16), ((1024, 512), BF16), ((512, 1024), BF16),
        ((1024, 256), BF16), ((1024, 256), BF16), ((1024, 256), BF16), ((1024, 256), BF16),
        ((256, 256), BF16), ((256, 256), BF16), ((256, 256), BF16), ((256, 256), BF16),
        ((4, 128, 128), F32), ((4, 128, 128), F32),
        ((1024, 256), BF16), ((1024, 128), BF16), ((1024, 128), BF16), ((1024, 1024), F32),
        ((1024, 1024), BF16), ((1024, 1024), BF16), ((128, 1024), BF16), ((128, 1024), BF16),
        ((1, 1024), F32), ((128, 1024), BF16), ((1024, 256), BF16), ((1024, 256), BF16),
        ((256, 128), BF16), ((256, 128), BF16), ((256, 128), BF16), ((256, 512), BF16),
        ((2, 128, 256), BF16), ((1024, 256), BF16), ((1024, 512), BF16), ((256, 512), BF16),
        ((256, 512), BF16), ((4, 8, 512), F32), ((4, 8, 512), F32), ((128, 128), BF16),
        ((128, 2048), BF16), ((8, 2048), F32),
    ]
    shapes = (
        jax.ShapeDtypeStruct((128, 1024), BF16),
        jax.ShapeDtypeStruct((128, 1024), BF16),
        jax.ShapeDtypeStruct((128, 128), BF16),
        jax.ShapeDtypeStruct((128, 2048), BF16),
        jax.ShapeDtypeStruct((8, 2048), F32),
    )
    results = pl.pallas_call(
        kernel,
        out_shape=shapes,
        in_specs=[vmem] * 3 + [hbm] * 5,
        out_specs=(hbm,) * 5,
        scratch_shapes=[pltpu.VMEM(shape, dtype) for shape, dtype in scratch]
        + [
            pltpu.SemaphoreType.DMA((10,)),
            pltpu.SemaphoreType.DMA((PHASES,)),
            pltpu.SemaphoreType.DMA((PHASES,)),
            pltpu.SemaphoreType.DMA((2, 8)),
        ],
        compiler_params=pltpu.CompilerParams(
            collective_id=0, has_side_effects=True, vmem_limit_bytes=62 * 1024 * 1024
        ),
    )(plan.T, lengths, freq, tokens, queries, values, out_grad, key_weight)
    return pl.pallas_call(
        copy_out,
        out_shape=shapes,
        in_specs=[hbm] * 5,
        out_specs=(hbm,) * 5,
        scratch_shapes=[pltpu.VMEM(item.shape, item.dtype) for item in shapes]
        + [pltpu.SemaphoreType.DMA((2, 5))],
        compiler_params=pltpu.CompilerParams(vmem_limit_bytes=62 * 1024 * 1024),
    )(*results)


def solution(mesh):
    both = P(("dp", "ctx"), "tensor")
    return jax.shard_map(
        shards,
        mesh=mesh,
        in_specs=(both, both, both, both, P(None, "tensor"), P(), P()),
        out_specs=(both,) * 5,
        check_vma=False,
    )
```

time: 129 us -> 103 us (0.80)
  Pallas kernels: 117 us -> 103 us
  local copies, waits for them, and re-layouts: 10.9 us -> 0 us
    pallas_call x1 -> x2, Pallas kernels: 117 us -> 103 us  [the longest x1 100 us: shards(): pl.pallas_call(kernel, out_shape=shapes, in_specs=[vmem] * 3 + [hbm] * 5,...]
    unnamed x20 -> x0, local copies, waits for them, and re-layouts: 10.9 us -> none
where the time goes in v3:
time: 103 us
  Pallas kernels  103 us (100%)
    pallas_call x1, Pallas kernels, shards(): pl.pallas_call(kernel, out_shape=shapes, in_specs=[vmem] * 3 + [hbm] * 5,...  100 us
    pallas_call x1, Pallas kernels, shards(): pl.pallas_call(copy_out, out_shape=shapes, in_specs=[hbm] * 5, out_specs=...  2.11 us

profile of v3, /device:TPU:2, one launch (start us, length us, event | category | flops | bytes accessed | tf_op | source)
XLA Modules:
  0.0 103.2 jit_solution(17656116074878405553)
XLA Ops:
  0.6 100.4 %shard_map.119 = (bf16[128,1024]{1,0:T(8,128)(2,1)}, bf16[128,1024]{1,0:T(8,128)(2,1)}, bf16[128,128]{1,0:T(8,128)(2,1)}, bf16[128,2048]{1,0:T(8,128)(2,1)}, f32[8,2048]{1,0:T(8,128)}) custom-call(s32[32,64]{1,0:T(8,128)} %bitcast.1, s32[8,16]{1,0:T(8,128)} %lengths.1, f32[1,128]{1,0:T(1,128)} %constant.2.clone.freq, bf16[128,2048]{1,0:T(8,128)(2,1)} %tokens_h.1, ...), custom_call_target="tpu_custom_call" | custom-call | tf_op jit(solution)/shard_map/pallas_call | solution.py:552
  101.1 2.1 %shard_map.120 = (bf16[128,1024]{1,0:T(8,128)(2,1)}, bf16[128,1024]{1,0:T(8,128)(2,1)}, bf16[128,128]{1,0:T(8,128)(2,1)}, bf16[128,2048]{1,0:T(8,128)(2,1)}, f32[8,2048]{1,0:T(8,128)}) custom-call(bf16[128,1024]{1,0:T(8,128)(2,1)} %get-tuple-element.10.refs_0_, bf16[128,1024]{1,0:T(8,128)(2,1)} %get-tuple-element.11.refs_1_, ...), custom_call_target="tpu_custom_call" | custom-call | tf_op jit(solution)/shard_map/pallas_call | solution.py:568

commit v4 on v3

--- a/solution.py
+++ b/solution.py
@@ -11,9 +11,10 @@
 F32, BF16 = jnp.float32, jnp.bfloat16
 HEAD = 128
 THETA = 500000.0
+LOG2E = math.log2(math.e)
 MESH = pl.DeviceIdType.MESH
-Q, ZKV, CKV, DO, PART, GATHER, TERMS, ZBACK, CBACK, KEYS, TOK, ZSUM, YSUM = range(13)
-PHASES = 13
+Q, ZKV, CKV, DO, PART, GATHER, BACK, KEYS, HEADS, TOK, ZSUM = range(11)
+PHASES = 11
 L_TOK, L_W, L_Q, L_V, L_DO, L_ATT, L_QG, L_VG, L_FG, L_KWG = range(10)
 
 
@@ -46,8 +47,9 @@
     att_h, qg_h, vg_h, fg_h, kwg_h,
     tok, qv, vv, dov, wv, smat, rmat,
     send_q, recv_q, send_do, recv_do, zkv_s, zkv_r, ckv_s, ckv_r, part_s, part_r,
-    kv_all, qs, dos, prob, weights, dscores, att, att_t, delta, qg, terms_s, terms_r,
-    zs, zr, cs, cr, kgs, kgr, toks, sum_s, sum_r, ys, yr, vg, fg, kwg,
+    kv_all, key_t, value_t, qs, dos, prob, weights, dscores, att, att_t, delta, qg,
+    terms_s, terms_r, back, collect, back_s, back_r, kgs, kgr, toks, sum_s, sum_r,
+    fg_s, fg_r, vg, fg, kwg,
     local_sem, send_sem, recv_sem, term_sem,
 ):
     d, c, t = lax.axis_index("dp"), lax.axis_index("ctx"), lax.axis_index("tensor")
@@ -106,12 +108,11 @@
         DO: recv_do.at[pl.ds(0, 1008)],
         PART: part_r.at[pl.ds(0, 3)],
         GATHER: kv_all.at[pl.ds(0, 896)],
-        ZBACK: zr.at[pl.ds(0, 224)],
-        CBACK: kgr.at[pl.ds(0, 496)],
-        KEYS: kgr.at[pl.ds(0, 896)],
-        TOK: toks.at[pl.ds(0, 896)],
-        ZSUM: sum_r.at[pl.ds(0, 224)],
-        YSUM: yr.at[pl.ds(0, 3)],
+        BACK: back_r.at[pl.ds(0, 1008)],
+        KEYS: kgr.at[pl.ds(0, 496)],
+        HEADS: fg_r.at[pl.ds(0, 96)],
+        TOK: toks.at[:, pl.ds(0, 448)],
+        ZSUM: sum_r.at[pl.ds(0, 496)],
     }
     unsent, unread = set(), set()
 
@@ -164,29 +165,11 @@
 
     loads.pop(L_Q).wait()
     send_q[...] = stage(qv)
-    pl.semaphore_wait(barrier, 87)
-
-    def send_slots(source, target, phase):
-        def one(k, carry):
-            peer = lax.rem(me + k, 64)
-            remote(
-                source.at[rows(peer * 16, 16, 16), :],
-                target.at[rows(me * 16, 16, 16), :],
-                phase,
-                (lax.div(peer, 8), lax.rem(peer, 8), t),
-            ).start()
-            return carry
-
-        lax.fori_loop(1, 64, one, 0)
-        started(phase)
-        target[rows(me * 16, 16, 16), :] = source[rows(me * 16, 16, 16), :]
-
-    send_slots(send_q, recv_q, Q)
-
     loads.pop(L_TOK).wait()
     loads.pop(L_W).wait()
     for h in range(4):
         part_s[h] = mm_nt(tok[...], wv[h * 128 : h * 128 + 128, :])
+    pl.semaphore_wait(barrier, 87)
 
     def send_part(k, carry):
         tt = lax.rem(t + k, 4)
@@ -197,6 +180,47 @@
     started(PART)
     part_r[pl.ds(t, 1)] = part_s[pl.ds(t, 1)]
 
+    def far_first(k, places):
+        m = lax.rem(k, 8)
+        near = lax.div(m + 1, 2)
+        ahead = jnp.where(lax.rem(m, 2) == 1, 4 - near, 4 + near)
+        return lax.rem(d + ahead, 8), lax.rem(lax.div(k, 8) + m + 2, places)
+
+    def send_slots(source, target, phase, low, high):
+        def one(k, carry):
+            g, away = far_first(k, 8)
+            cc = lax.rem(c + away, 8)
+            remote(
+                source.at[rows((g * 8 + cc) * 16, 16, 16), :],
+                target.at[rows(me * 16, 16, 16), :],
+                phase,
+                (g, cc, t),
+            ).start()
+            return carry
+
+        lax.fori_loop(low, high, one, 0)
+
+    def own_slot(source, target):
+        target[rows(me * 16, 16, 16), :] = source[rows(me * 16, 16, 16), :]
+
+    send_slots(send_q, recv_q, Q, 0, 32)
+
+    def send_tokens(k, carry):
+        cc = lax.rem(c + k, 8)
+        for part in range(2):
+            remote(
+                tok.at[pl.ds(part * 64, 64), rows(lax.rem(cc, 4) * 512, 512, 128)],
+                toks.at[part, rows(c * 64, 64, 64), :],
+                TOK,
+                (d, cc, t),
+            ).start()
+        return carry
+
+    lax.fori_loop(1, 3, send_tokens, 0)
+    for part in range(2):
+        toks[part, rows(c * 64, 64, 64), :] = tok[
+            part * 64 : part * 64 + 64, rows(y * 512, 512, 128)
+        ]
     line, column = iota((256, 128), 0), iota((256, 128), 1)
     four = lax.rem(line, 4) == lax.rem(column, 4)
     to_slots = one_hot(four & (dest[:, 0:128] == lax.div(line, 4).astype(F32)))
@@ -242,7 +266,7 @@
 
     def send_blocks(source, target, phase, size):
         def one(k, carry):
-            g = lax.rem(d + k, 8)
+            g = far_first(k, 8)[0]
             remote(
                 source.at[rows(g * size, size, size), :],
                 target.at[rows(d * size, size, size), :],
@@ -251,12 +275,15 @@
             ).start()
             return carry
 
-        lax.fori_loop(1, 8, one, 0)
+        lax.fori_loop(0, 7, one, 0)
         started(phase)
         target[rows(d * size, size, size), :] = source[rows(d * size, size, size), :]
 
     send_blocks(zkv_s, zkv_r, ZKV, 32)
-    send_slots(send_do, recv_do, DO)
+    send_slots(send_q, recv_q, Q, 32, 63)
+    started(Q)
+    own_slot(send_q, recv_q)
+    own_slot(send_do, recv_do)
 
     slot = lax.div(iota((64, 1024), 1), 16)
     col = iota((128, 1024), 1)
@@ -282,6 +309,7 @@
     lax.fori_loop(1, 8, send_ckv, 0)
     started(CKV)
     ckv_r[rows(c * 32, 32, 32), :] = ckv_s[rows(c * 32, 32, 32), :]
+    send_slots(send_do, recv_do, DO, 0, 16)
     for k in range(8):
 
         @pl.when(k < c)
@@ -303,20 +331,12 @@
 
     lax.fori_loop(1, 8, send_gather, 0)
     started(GATHER)
-
-    def send_tokens(k, carry):
-        cc = lax.rem(c + k, 8)
-        remote(
-            tok.at[:, rows(lax.rem(cc, 4) * 512, 512, 128)],
-            toks.at[rows(c * 128, 128, 128), :],
-            TOK,
-            (d, cc, t),
-        ).start()
-        return carry
-
-    lax.fori_loop(1, 8, send_tokens, 0)
-    started(TOK)
-    toks[rows(c * 128, 128, 128), :] = tok[:, rows(y * 512, 512, 128)]
+    send_slots(send_do, recv_do, DO, 16, 63)
+    started(DO)
+
+    lax.fori_loop(3, 6, send_tokens, 0)
+    back[...] = rmat[0:128, :].T
+    collect[...] = smat[:, 0:128].T
 
     arrived(Q)
     heads = mm(rmat[...], recv_q[...]).astype(BF16)
@@ -343,21 +363,26 @@
     hidden = jnp.where((key_at <= query_at[0:1]) & (key_at >= starts), 0.0, -1e30)
 
     arrived(GATHER)
+    key_t[...] = kv_all[:, 0:128].T
+    value_t[...] = kv_all[:, 128:256].T
+
+    hidden = jnp.concatenate([hidden, hidden], axis=1)
 
     def forward(h, carry):
-        here = rows(h * 128, 128, 128)
-        scores = mm_nt(kv_all[:, 0:128], qs[here, :]) * scale + hidden
-        grown = jnp.exp(scores - jnp.max(scores, axis=0, keepdims=True))
+        here = rows(h * 256, 256, 256)
+        scores = mm_nt(kv_all[:, 0:128], qs[here, :]) * (scale * LOG2E) + hidden
+        grown = jnp.exp2(scores - jnp.max(scores, axis=0, keepdims=True))
         chance = grown * (1.0 / jnp.sum(grown, axis=0, keepdims=True))
         prob[:, here] = chance
         rounded = chance.astype(BF16)
         weights[:, here] = rounded
-        out = mm_tn(kv_all[:, 128:256], rounded).astype(BF16)
+        out = mm(value_t[...], rounded).astype(BF16)
         att_t[:, here] = out
-        att[:, here] = out.T
-        return carry
-
-    lax.fori_loop(0, 8, forward, 0)
+        for k in range(2):
+            att[:, rows(h * 256 + k * 128, 128, 128)] = out[:, k * 128 : k * 128 + 128].T
+        return carry
+
+    lax.fori_loop(0, 4, forward, 0)
     stores[L_ATT] = local(att, att_h, L_ATT)
     stores[L_ATT].start()
 
@@ -365,11 +390,11 @@
     heads = mm(rmat[...], recv_do[...]).astype(BF16)
     for ch in range(4):
         for k in range(2):
-            h = 2 * ch + k
+            low = (2 * ch + k) * 128
             block = heads[ch * 128 : ch * 128 + 128, k * 128 : k * 128 + 128]
-            dos[h * 128 : h * 128 + 128, :] = block
-            products = block.T.astype(F32) * att_t[:, h * 128 : h * 128 + 128].astype(F32)
-            delta[:, h * 128 : h * 128 + 128] = jnp.sum(products, axis=0, keepdims=True)
+            dos[low : low + 128, :] = block
+            products = block.T.astype(F32) * att_t[:, low : low + 128].astype(F32)
+            delta[:, low : low + 128] = jnp.sum(products, axis=0, keepdims=True)
 
     def backward(k, carry):
         chunk = lax.rem(lax.div(c, 2) + 1 + k, 4)
@@ -392,34 +417,15 @@
     terms_r[rows(c * 128, 128, 128), :] = terms_s[rows(c * 128, 128, 128), :]
 
     def query_grads(h, carry):
-        here = rows(h * 128, 128, 128)
-        grad = mm_tn(kv_all[:, 0:128], dscores[:, here]) * scale
-        qg[:, here] = grad.astype(BF16).T
-        return carry
-
-    lax.fori_loop(0, 8, query_grads, 0)
+        grad = (mm(key_t[...], dscores[:, rows(h * 256, 256, 256)]) * scale).astype(BF16)
+        for k in range(2):
+            qg[:, rows(h * 256 + k * 128, 128, 128)] = grad[:, k * 128 : k * 128 + 128].T
+        return carry
+
+    lax.fori_loop(0, 4, query_grads, 0)
     stores[L_QG] = local(qg, qg_h, L_QG)
     stores[L_QG].start()
 
-    before = mm(one_hot(iota((64, 64), 1) < iota((64, 64), 0)), live_col).astype(BF16)
-    widen = one_hot(iota((256, 64), 1) == lax.div(iota((256, 64), 0), 4))
-    spot = mm(widen, before) * 4.0 + lax.rem(line, 4).astype(F32)
-    spot = jnp.where(mm(widen, live_col) > 0.5, spot, -1.0)
-    back = one_hot(spot == column.astype(F32))
-    spread4 = one_hot(iota((128, 32), 1) == lax.div(iota((128, 32), 0), 4))
-    lane = iota((128, 256), 1)
-    sender = lax.div(lax.rem(lane, 32), 4) * 8 + lax.div(lane, 32)
-    collect = one_hot(
-        (mm(spread4, row) == sender.astype(F32))
-        & (lax.rem(lane, 4) == lax.rem(iota((128, 256), 0), 4))
-    )
-    new_col, old = iota((512, 512), 1), iota((512, 512), 0)
-    reorder = one_hot(
-        old
-        == lax.div(lax.rem(new_col, 256), 32) * 64
-        + lax.div(new_col, 256) * 32
-        + lax.rem(new_col, 32)
-    )
     for k in range(8):
 
         @pl.when(k > c)
@@ -431,73 +437,88 @@
         owned += terms_r[k * 128 : k * 128 + 128, :].astype(F32)
     rot_grad = owned[:, 0:128] * scale
     key_grad = (rot_grad * cosine - pltpu.roll(rot_grad, 64, 1) * signed).astype(BF16)
-    zs[...] = mm(back, key_grad).astype(BF16)
-    send_blocks(zs, zr, ZBACK, 32)
+    back_s[...] = mm(back[...], key_grad).astype(BF16)
+    send_slots(back_s, back_r, BACK, 0, 63)
+    started(BACK)
+    own_slot(back_s, back_r)
+    lax.fori_loop(6, 8, send_tokens, 0)
+    started(TOK)
     vg[...] = owned[:, 128:256].astype(BF16)
     stores[L_VG] = local(vg, vg_h, L_VG)
     stores[L_VG].start()
-    arrived(ZBACK)
-    cs[...] = mm(regroup, zr[...]).astype(BF16)
-
-    def send_c(k, carry):
+    old, new_col = iota((128, 256), 0), iota((128, 256), 1)
+    packed = (lax.div(lax.rem(old, 64), 32) == lax.div(new_col, 128)) & (
+        lax.div(old, 64) * 32 + lax.rem(old, 32) == lax.rem(new_col, 64)
+    )
+    upper_rows = lax.rem(new_col, 128) < 64
+    pack_a, pack_b = one_hot(packed & upper_rows), one_hot(packed & ~upper_rows)
+    arrived(BACK)
+    own_grads = mm(collect[...], back_r[...]).astype(BF16)
+
+    moved = (mm(own_grads[0:64], pack_a) + mm(own_grads[64:128], pack_b)).astype(BF16)
+    for k in range(2):
+        kgs[k] = moved[:, k * 128 : k * 128 + 128]
+
+    def send_grads(k, carry):
         cc = lax.rem(c + k, 8)
         tt = lax.rem(t + lax.div(k, 8), 4)
         remote(
-            cs.at[rows(cc * 32, 32, 32), :],
-            cr.at[rows(c * 32, 32, 32), rows(t * 128, 128, 128)],
-            CBACK,
+            kgs.at[lax.div(cc, 4)],
+            kgr.at[rows(c * 64, 64, 64), rows(t * 128, 128, 128)],
+            KEYS,
             (d, cc, tt),
         ).start()
         return carry
 
-    lax.fori_loop(1, 32, send_c, 0)
-    started(CBACK)
-    cr[rows(c * 32, 32, 32), rows(t * 128, 128, 128)] = cs[rows(c * 32, 32, 32), :]
-    arrived(CBACK)
-    all_grads = mm(collect, cr[...]).astype(BF16)
-
-    moved = mm(all_grads, reorder).astype(BF16)
-    for k in range(2):
-        kgs[k] = moved[:, k * 256 : k * 256 + 256]
-
-    def send_grads(k, carry):
-        cc = lax.rem(c + k, 8)
+    lax.fori_loop(1, 32, send_grads, 0)
+    started(KEYS)
+    kgr[rows(c * 64, 64, 64), rows(t * 128, 128, 128)] = kgs[x]
+    fg_s[...] = own_grads
+
+    def send_heads(k, carry):
+        tt = lax.rem(t + k, 4)
+        remote(fg_s, fg_r.at[:, rows(t * 128, 128, 128)], HEADS, (d, c, tt)).start()
+        return carry
+
+    lax.fori_loop(1, 4, send_heads, 0)
+    started(HEADS)
+    fg_r[:, rows(t * 128, 128, 128)] = own_grads
+    arrived(TOK)
+    arrived(KEYS)
+    turned = kgr[...].T
+    even = jnp.concatenate([turned[k * 128 : k * 128 + 64] for k in range(4)], axis=0)
+    odd = jnp.concatenate([turned[k * 128 + 64 : k * 128 + 128] for k in range(4)], axis=0)
+    part = mm(even, toks[0]) + mm(odd, toks[1])
+    pieces = [part[:, k * 256 : k * 256 + 256].reshape(32, 1, 8, 256) for k in range(2)]
+    sum_s[...] = jnp.concatenate(pieces, axis=1).reshape(512, 256).astype(BF16)
+
+    def send_sums(k, carry):
+        g, away = far_first(k, 4)
+        yy = lax.rem(y + away, 4)
         remote(
-            kgs.at[lax.div(cc, 4)], kgr.at[rows(c * 128, 128, 128), :], KEYS, (d, cc, t)
+            sum_s.at[rows((g * 4 + yy) * 16, 16, 16), :],
+            sum_r.at[rows((d * 4 + y) * 16, 16, 16), :],
+            ZSUM,
+            (g, x * 4 + yy, t),
         ).start()
         return carry
 
-    lax.fori_loop(1, 8, send_grads, 0)
-    started(KEYS)
-    kgr[rows(c * 128, 128, 128), :] = kgs[x]
+    lax.fori_loop(0, 31, send_sums, 0)
+    started(ZSUM)
+    sum_r[rows((d * 4 + y) * 16, 16, 16), :] = sum_s[rows((d * 4 + y) * 16, 16, 16), :]
+    arrived(HEADS)
     for k in range(4):
         fg[:, k * 512 : k * 512 + 512] = mm(
-            all_grads, wv[:, k * 512 : k * 512 + 512]
+            fg_r[...], wv[:, k * 512 : k * 512 + 512]
         ).astype(BF16)
     stores[L_FG] = local(fg, fg_h, L_FG)
     stores[L_FG].start()
-    arrived(TOK)
-    arrived(KEYS)
-    sum_s[...] = mm_tn(kgr[...], toks[...]).astype(BF16)
-    send_blocks(sum_s, sum_r, ZSUM, 32)
     arrived(ZSUM)
-    added = sum_r[0:32, :].astype(F32)
+    added = sum_r[0:64, :].astype(F32)
     for k in range(1, 8):
-        added += sum_r[k * 32 : k * 32 + 32, :].astype(F32)
-    for k in range(4):
-        ys[k] = added[k * 8 : k * 8 + 8]
-
-    def send_y(k, carry):
-        yy = lax.rem(y + k, 4)
-        remote(ys.at[yy], yr.at[y], YSUM, (d, x * 4 + yy, t)).start()
-        return carry
-
-    lax.fori_loop(1, 4, send_y, 0)
-    started(YSUM)
-    yr[y] = ys[y]
-    arrived(YSUM)
-    for k in range(4):
-        kwg[:, k * 512 : k * 512 + 512] = yr[k]
+        added += sum_r[k * 64 : k * 64 + 64, :].astype(F32)
+    for k in range(8):
+        kwg[:, k * 256 : k * 256 + 256] = added[k * 8 : k * 8 + 8]
     stores[L_KWG] = local(kwg, kwg_h, L_KWG)
     stores[L_KWG].start()
     for k in range(8):
@@ -534,13 +555,14 @@
         ((1024, 256), BF16), ((1024, 256), BF16), ((1024, 256), BF16), ((1024, 256), BF16),
         ((256, 256), BF16), ((256, 256), BF16), ((256, 256), BF16), ((256, 256), BF16),
         ((4, 128, 128), F32), ((4, 128, 128), F32),
-        ((1024, 256), BF16), ((1024, 128), BF16), ((1024, 128), BF16), ((1024, 1024), F32),
-        ((1024, 1024), BF16), ((1024, 1024), BF16), ((128, 1024), BF16), ((128, 1024), BF16),
-        ((1, 1024), F32), ((128, 1024), BF16), ((1024, 256), BF16), ((1024, 256), BF16),
-        ((256, 128), BF16), ((256, 128), BF16), ((256, 128), BF16), ((256, 512), BF16),
-        ((2, 128, 256), BF16), ((1024, 256), BF16), ((1024, 512), BF16), ((256, 512), BF16),
-        ((256, 512), BF16), ((4, 8, 512), F32), ((4, 8, 512), F32), ((128, 128), BF16),
-        ((128, 2048), BF16), ((8, 2048), F32),
+        ((1024, 256), BF16), ((128, 1024), BF16), ((128, 1024), BF16), ((1024, 128), BF16),
+        ((1024, 128), BF16), ((1024, 1024), F32), ((1024, 1024), BF16), ((1024, 1024), BF16),
+        ((128, 1024), BF16), ((128, 1024), BF16), ((1, 1024), F32), ((128, 1024), BF16),
+        ((1024, 256), BF16), ((1024, 256), BF16), ((1024, 128), BF16),
+        ((128, 1024), BF16), ((1024, 128), BF16), ((1024, 128), BF16), ((2, 64, 128), BF16),
+        ((512, 512), BF16), ((2, 512, 512), BF16), ((512, 256), BF16), ((512, 256), BF16),
+        ((128, 128), BF16), ((128, 512), BF16), ((128, 128), BF16), ((128, 2048), BF16),
+        ((8, 2048), F32),
     ]
     shapes = (
         jax.ShapeDtypeStruct((128, 1024), BF16),

time: 103 us -> 92.8 us (0.901)
  the two profiles are of different devices: /device:TPU:2 before, /device:TPU:1 now
where the time goes in v4:
time: 92.8 us; the launch traced here: 92.7 us
  Pallas kernels  92 us (99%)
    pallas_call x1, Pallas kernels, shards(): pl.pallas_call(kernel, out_shape=shapes, in_specs=[vmem] * 3 + [hbm] * 5,...  89.9 us
    pallas_call x1, Pallas kernels, shards(): pl.pallas_call(copy_out, out_shape=shapes, in_specs=[hbm] * 5, out_specs=...  2.11 us

profile of v4, /device:TPU:1, one launch (start us, length us, event | category | flops | bytes accessed | tf_op | source)
XLA Modules:
  0.0 92.7 jit_solution(2161838697682564629)
XLA Ops:
  0.6 89.9 %shard_map.119 = (bf16[128,1024]{1,0:T(8,128)(2,1)}, bf16[128,1024]{1,0:T(8,128)(2,1)}, bf16[128,128]{1,0:T(8,128)(2,1)}, bf16[128,2048]{1,0:T(8,128)(2,1)}, f32[8,2048]{1,0:T(8,128)}) custom-call(s32[32,64]{1,0:T(8,128)} %bitcast.1, s32[8,16]{1,0:T(8,128)} %lengths.1, f32[1,128]{1,0:T(1,128)} %constant.2.clone.freq, bf16[128,2048]{1,0:T(8,128)(2,1)} %tokens_h.1, ...), custom_call_target="tpu_custom_call" | custom-call | tf_op jit(solution)/shard_map/pallas_call | solution.py:574
  90.6 2.1 %shard_map.120 = (bf16[128,1024]{1,0:T(8,128)(2,1)}, bf16[128,1024]{1,0:T(8,128)(2,1)}, bf16[128,128]{1,0:T(8,128)(2,1)}, bf16[128,2048]{1,0:T(8,128)(2,1)}, f32[8,2048]{1,0:T(8,128)}) custom-call(bf16[128,1024]{1,0:T(8,128)(2,1)} %get-tuple-element.10.refs_0_, bf16[128,1024]{1,0:T(8,128)(2,1)} %get-tuple-element.11.refs_1_, ...), custom_call_target="tpu_custom_call" | custom-call | tf_op jit(solution)/shard_map/pallas_call | solution.py:590
